TPU v7x, 32 devices: a whole 2x2x4 slice. The times are simulated.
32 devices in a mesh: ref: 8 (over z, x), voc: 4 (over y, core).
Axes of the slice: x: 2, y: 2, z: 4, core: 2. Of those that a mesh axis runs over, the one named last changes fastest.
Arguments:
- private_logits: bfloat16 [96, 4, 128256], P('ref', None, 'voc'), may hold values from -16 to 16
- public_logits: bfloat16 [4, 4, 128256], P(None, None, ('voc', 'ref')), may hold values from -250 to 250
- noise: bfloat16 [4, 4, 128256], P(None, None, ('voc', 'ref')), may hold values from -6 to 6
- owner: int32 [96], P('ref'), may hold values from 0 to 3, as said below
- counts: int32 [4], replicated, may hold values from 1 to 24, as said below
- tokens: int32 [4, 4], replicated, may hold values from 0 to 128255
Outputs:
- logprobs: float32 [4, 4, 128256], P(None, None, ('voc', 'ref'))
- target: float32 [4, 4], replicated
Inputs may be any that keep to these rules, and one draw needn't show every extreme that they name: `owner`: each of the 4 texts owns exactly 24 rows. `counts`: the count of a text is at least half of the rows that it owns, rounded up, and at most all of them; some text keeps all of its rows.
All inputs are finite; a program needn't handle non-finite values.
Results may differ from a plain program's by a relative error of at most 0.0003.
Values may be sent and summed in bfloat16 or wider, within the bound.
A program may use at most 128 MiB of HBM per device.

v0:
```python
import jax
import jax.numpy as jnp
from jax import lax
from jax.sharding import PartitionSpec as P

clip_bound = 2.0


def prefix(x, axis, combine, identity):
    peers, index = (lax.axis_size(axis), lax.axis_index(axis))
    everything = lax.all_gather(x, axis)
    start = jnp.broadcast_to(jnp.asarray(identity, x.dtype), x.shape)

    def lap(k, before):
        reached = k < index
        new = combine(before, everything[k])
        return jnp.where(reached, new, before)

    return lax.fori_loop(0, peers, lap, start)


def add_counts(earlier, later):
    return earlier + later


def wide_stats(combined, picked_local):
    row_peak = lax.pmax(jnp.max(combined, axis=2), ("ref", "voc"))
    row_total, picked = lax.psum(
        (jnp.sum(jnp.exp(combined - row_peak[:, :, None]), axis=2), picked_local), ("ref", "voc")
    )
    return (row_peak, row_total, picked)


def pick_tokens(combined, first_column, tokens):
    column = first_column + jnp.arange(combined.shape[2], dtype=jnp.int32)
    return jnp.sum(jnp.where(column[None, None, :] == tokens[:, :, None], combined, 0.0), axis=2)


def body(private_logits, public_logits, noise, owner, counts, tokens):
    text_count = counts.shape[0]
    labels = jnp.arange(text_count, dtype=jnp.int32)
    chosen = (owner[:, None] == labels[None, :]).astype(jnp.int32)
    offset = prefix(jnp.sum(chosen, 0), "ref", add_counts, jnp.zeros((text_count,), jnp.int32))
    before = jnp.cumsum(chosen, 0) - chosen
    row_rank = jnp.sum((before + offset[None, :]) * chosen, 1)
    row_limit = jnp.sum(chosen * counts[None, :], 1)
    select = chosen.astype(jnp.float32)
    weight = select * (row_rank < row_limit).astype(jnp.float32)[:, None]
    text_scale = 1.0 / (clip_bound * jnp.sqrt(counts.astype(jnp.float32)))
    matched = jnp.einsum(
        "rt,tpv->rpv",
        select,
        lax.all_gather(public_logits, "ref", axis=2, tiled=True).astype(jnp.float32),
        precision=lax.Precision.HIGHEST,
    )
    clipped = jnp.clip(private_logits.astype(jnp.float32) - matched, -clip_bound, clip_bound)
    partial_sums = jnp.einsum("rt,rpv->tpv", weight, clipped, precision=lax.Precision.HIGHEST)
    summed = lax.psum_scatter(partial_sums, "ref", scatter_dimension=2, tiled=True)
    combined = (
        public_logits.astype(jnp.float32)
        + summed * text_scale[:, None, None]
        + noise.astype(jnp.float32)
    )
    block_width = combined.shape[2]
    first_column = (
        lax.axis_index("voc") * lax.axis_size("ref") + lax.axis_index("ref")
    ) * block_width
    row_peak, row_total, picked = wide_stats(combined, pick_tokens(combined, first_column, tokens))
    lse = row_peak + jnp.log(row_total)
    logprobs = combined - lse[:, :, None]
    target = picked - lse
    return (logprobs, target)


def solution(mesh):
    return jax.shard_map(
        body,
        mesh=mesh,
        in_specs=(
            P("ref", None, "voc"),
            P(None, None, ("voc", "ref")),
            P(None, None, ("voc", "ref")),
            P("ref"),
            P(),
            P(),
        ),
        out_specs=(P(None, None, ("voc", "ref")), P()),
        check_vma=False,
    )
```

profile of v0, /device:TPU:0, one launch (start us, length us, event | category | flops | bytes accessed | tf_op | source)
XLA Modules:
  0.0 889.0 jit_solution(350615721629046309)
XLA Ops:
  7.2 0.0 all-reduce.5.cloned.1.call-start
  7.2 5.6 copy.24
  12.8 621.5 %all_gather.11 = bf16[4,4,32064]{1,0,2:T(4,128)(2,1)} all-gather(bf16[4,4,4008]{1,0,2:T(4,128)(2,1)} %copy.24), channel_id=1, replica_groups=mesh['ref'=8,'voc'=4] {'ref'}, dimensions={2}, use_global_device_ids=true | all-gather | bytes 1154304 | tf_op jit(solution)/shard_map/all_gather | solution.py:53
  634.3 0.0 copy-start.3
  634.3 0.0 copy-start.6
  634.3 0.0 copy-start.4
  634.3 0.0 copy-start
  634.4 41.7 %copy.25 = bf16[4,4,32064]{2,0,1:T(4,128)(2,1)} copy(bf16[4,4,32064]{1,0,2:T(4,128)(2,1)} %all_gather.11) | data formatting | bytes 2052096 | tf_op jit(solution)/shard_map/all_gather | solution.py:53
  676.1 0.0 copy-done.3
  676.1 0.2 reduce_window_sum.11
  676.3 0.0 copy-done.6
  676.3 0.1 select_reduce_fusion.1
  676.4 0.0 copy-done.4
  676.4 0.7 fusion.19
  677.8 0.2 dynamic-update-slice
  678.1 10.6 %all-reduce = s32[32]{0:T(128)S(1)} all-reduce(s32[32]{0:T(128)S(1)} %dynamic-update-slice), channel_id=2, replica_groups=mesh['ref'=8,'voc'=4] {'ref'}, use_global_device_ids=true, to_apply=%add | all-reduce | flops 32 | bytes 256
  688.7 0.1 reshape.21
  688.7 0.3 while.14
  689.0 0.0 copy-done
  689.0 5.7 fusion
  694.8 0.0 copy-start.5
  694.8 0.0 copy-start.1
  694.8 0.0 copy-start.2
  694.8 0.1 fusion.11
  694.9 5.1 fusion.6
  700.1 0.0 all-reduce.5.cloned.1.call-update
  700.1 0.0 copy-done.5
  700.1 0.1 copy.27
  700.9 98.9 %all-reduce.5.cloned.1.call-done = f32[4,4,32064]{2,0,1:T(4,128)} async-done(((f32[4,4,32064]{2,0,1:T(4,128)}), f32[4,4,32064]{2,0,1:T(4,128)}) %all-reduce.5.cloned.1.call-update) | async-done | bytes 2052112
  799.8 0.0 copy-done.1
  799.8 0.0 copy-done.2
  799.8 1.3 fusion.17
  801.0 40.1 %pmax.7 = f32[4,4]{0,1:T(4,128)S(1)} all-reduce(f32[4,4]{0,1:T(4,128)S(1)} %get-tuple-element.119), channel_id=1, replica_groups=mesh['ref'=8,'voc'=4] {'ref','voc'}, use_global_device_ids=true, to_apply=%region_8.9 | all-reduce | flops 16 | bytes 128 | tf_op jit(solution)/shard_map/pmax | solution.py:27
  841.1 0.3 select_reduce_fusion
  841.4 39.0 %all-reduce.2 = (f32[4,4]{0,1:T(4,128)S(1)}, f32[4,4]{0,1:T(4,128)S(1)}) all-reduce(f32[4,4]{0,1:T(4,128)S(1)} %get-tuple-element.104, f32[4,4]{0,1:T(4,128)S(1)} %get-tuple-element.103), channel_id=1, replica_groups=mesh['ref'=8,'voc'=4] {'ref','voc'}, use_global_device_ids=true, to_apply=%region_10.11 | all-reduce | flops 32 | bytes 256 | tf_op jit(solution)/shard_map/psum | solution.py:28
  880.5 0.1 broadcast_subtract_fusion
  880.6 0.9 copy.28
  881.5 0.7 copy.29
  (15 shorter events, 0.2 us)
Async XLA Ops:
  7.2 792.6 %all-reduce.5.cloned.1.call-start = ((), (), s32[]{:S(2)}) async-start(), calls=%async_computation | async-start | bytes 4112384
  634.3 41.8 %copy-start.3 = (s32[12]{0:T(128)S(1)}, s32[12]{0:T(128)}, u32[]{:S(2)}) copy-start(s32[12]{0:T(128)} %param.11) | copy-start | bytes 148
  634.3 42.0 %copy-start.6 = (s32[4]{0:T(128)S(1)}, s32[4]{0:T(128)}, u32[]{:S(2)}) copy-start(s32[4]{0:T(128)} %param.12) | copy-start | bytes 52
  634.3 42.1 %copy-start.4 = (u32[32]{0:T(128)S(1)}, u32[32]{0:T(128)}, u32[]{:S(2)}) copy-start(u32[32]{0:T(128)} %constant.60) | copy-start | bytes 388
  634.3 54.7 %copy-start = (bf16[12,4,32064]{2,1,0:T(4,128)(2,1)S(1)}, bf16[12,4,32064]{2,1,0:T(4,128)(2,1)}, u32[]{:S(2)}) copy-start(bf16[12,4,32064]{2,1,0:T(4,128)(2,1)} %param.8) | copy-start | bytes 9234436
  694.8 5.3 copy-start.5
  694.8 105.0 %copy-start.1 = (bf16[4,4,4008]{2,1,0:T(4,128)(2,1)S(1)}, bf16[4,4,4008]{2,1,0:T(4,128)(2,1)}, u32[]{:S(2)}) copy-start(bf16[4,4,4008]{2,1,0:T(4,128)(2,1)} %param.9) | copy-start | bytes 384772
  694.8 104.9 %copy-start.2 = (bf16[4,4,4008]{2,1,0:T(4,128)(2,1)S(1)}, bf16[4,4,4008]{2,1,0:T(4,128)(2,1)}, u32[]{:S(2)}) copy-start(bf16[4,4,4008]{2,1,0:T(4,128)(2,1)} %param.10) | copy-start | bytes 384772
Sparse Core Ops, SparseCore 0:
  700.2 99.5 all-reduce.4
where the time goes:
time: 891 us; the launch traced here: 889 us
  blocking collectives  711 us (80%)
  waiting for transfers between devices  98.9 us (11%)
  local copies, waits for them, and re-layouts  50 us (6%)
  between operations  15.5 us (2%)
  matrix products  10.9 us (1%)
    all_gather x1, blocking collectives, body(): lax.all_gather(public_logits, 'ref', axis=2, tiled=True).astype(jnp.float32)  622 us
    unnamed x2, waiting for transfers between devices  98.9 us
    all_gather x1, local copies, waits for them, and re-layouts, body(): lax.all_gather(public_logits, 'ref', axis=2, tiled=True).astype(jnp.float32)  41.7 us
    pmax x1, blocking collectives, wide_stats(): row_peak = lax.pmax(jnp.max(combined, axis=2), ('ref', 'voc'))  40.1 us
    psum x1, blocking collectives, wide_stats(): lax.psum((jnp.sum(jnp.exp(combined - row_peak[:, :, None]), axis=2), pick...  39 us
  transfers between devices with their start and end apart: 1, of which 1 were waited for; matrix products, arithmetic and copies ran while one was open for 0% of the time, Pallas kernels for 0%

commit v1 on v0

v1 whole, which is shorter than its diff:
```python
import functools

import jax
import jax.numpy as jnp
from jax import lax
from jax.experimental import pallas as pl
from jax.experimental.pallas import tpu as pltpu
from jax.sharding import PartitionSpec as P

clip_bound = 2.0
LANES = 128
MESH = pl.DeviceIdType.MESH


def fixed_point(rows):
    scale = 1
    while scale * 2 * clip_bound * rows <= 32000:
        scale *= 2
    return float(scale)


def kernel(
    n, nv, rows, texts, pos, width, piece, win,
    owner, counts, tokens, priv, pub, noise,
    combined_out, stats_out,
    pv, xt, pubf, pubs, here, pref, keep, snd1, rs1, snd2, rs2,
    hist, st1, st2, bnd, order, sown, start,
    priv_sem, hist_s, hist_r, ag_s, ag_f, ag_r, rs1_s, rs1_r, rs2_s, rs2_r,
    st1_s, st1_r, st2_s, st2_r,
):
    f32 = jnp.float32
    half = n // 2
    full = width // LANES
    wl = win * LANES
    me = lax.axis_index("ref")
    mv = lax.axis_index("voc")
    z = lax.div(me, 2)
    x = lax.rem(me, 2)
    partner = me + 1 - 2 * x
    scale1 = fixed_point(rows)
    scale2 = fixed_point(2 * rows)

    def first_tile(j):
        return jnp.minimum(lax.div(j * piece, LANES), full + 1 - win)

    def remote(src, dst, send, recv, peer):
        return pltpu.make_async_remote_copy(
            src_ref=src, dst_ref=dst, send_sem=send, recv_sem=recv,
            device_id=peer, device_id_type=MESH,
        )

    load = pltpu.make_async_copy(priv, pv, priv_sem)
    load.start()
    barrier = pltpu.get_barrier_semaphore()

    def greet(k, c):
        pl.semaphore_signal(barrier, inc=1, device_id={"ref": lax.rem(me + k, n)}, device_id_type=MESH)
        return c

    def greet_voc(k, c):
        pl.semaphore_signal(barrier, inc=1, device_id={"voc": lax.rem(mv + k, nv)}, device_id_type=MESH)
        return c

    lax.fori_loop(1, n, greet, 0)
    lax.fori_loop(1, nv, greet_voc, 0)

    shift = me * piece - first_tile(me) * LANES
    pubf[...] = jnp.zeros_like(pubf)
    for t in range(texts):
        pubf[t, :, :piece] = pub[t].astype(f32)
    for t in range(texts):
        pubs[me, t] = pltpu.roll(pubf[t], shift, 1).astype(jnp.bfloat16)

    own = [owner[r] for r in range(rows)]
    hits = [sum((o == t).astype(jnp.int32) for o in own) for t in range(texts)]
    begin = [jnp.int32(0)]
    for t in range(texts):
        begin.append(begin[-1] + hits[t])
    for t in range(texts + 1):
        start[t] = begin[t]
    place = []
    for r in range(rows):
        before = jnp.int32(0)
        for q in range(rows):
            if q < r:
                before = before + (own[q] <= own[r]).astype(jnp.int32)
            elif q > r:
                before = before + (own[q] < own[r]).astype(jnp.int32)
        place.append(before)
    for k in range(rows):
        at = jnp.int32(0)
        for r in range(rows):
            at = at + jnp.where(place[r] == k, r, 0)
        order[k] = at
        sown[k] = sum((begin[t] <= k).astype(jnp.int32) for t in range(1, texts))

    lane8 = lax.broadcasted_iota(jnp.int32, (8, LANES), 1)
    mine = jnp.zeros((8, LANES), jnp.int32)
    for t in range(texts):
        mine = jnp.where(lane8 == t, hits[t], mine)
    hist[me] = mine

    pl.semaphore_wait(barrier, n - 1 + nv - 1)

    def send_hist(k, c):
        remote(hist.at[me], hist.at[me], hist_s, hist_r, {"ref": lax.rem(me + k, n)}).start()
        return c

    lax.fori_loop(1, n, send_hist, 0)
    remote(pubs.at[me], pubs.at[me], ag_s.at[0], ag_r.at[me], {"ref": partner}).start()

    def send_own(k, c):
        peer = 2 * lax.rem(z + k, half) + x
        remote(pubs.at[me], pubs.at[me], ag_s.at[k], ag_r.at[me], {"ref": peer}).start()
        return c

    lax.fori_loop(1, half, send_own, 0)

    load.wait()
    for j in range(n):
        s = min(j * piece // LANES, full + 1 - win) + win - 1
        if s < full:
            xt[:, :, j * LANES:(j + 1) * LANES] = pv[:, :, s * LANES:(s + 1) * LANES]
        else:
            xt[:, :, j * LANES:(j + 1) * LANES] = jnp.zeros((rows, pos, LANES), jnp.bfloat16)
            if width > full * LANES:
                xt[:, :, j * LANES:j * LANES + width - full * LANES] = pv[:, :, full * LANES:]

    got = hist.at[pl.ds(0, n - 1)]
    pltpu.make_async_copy(got, got, hist_r).wait()
    pltpu.make_async_copy(got, got, hist_s).wait()
    lower = jnp.zeros((8, LANES), jnp.int32)
    lower = lax.fori_loop(0, n, lambda j, a: a + jnp.where(j < me, hist[j], 0), lower)
    lower = lower[:pos]
    lane4 = lax.broadcasted_iota(jnp.int32, (pos, LANES), 1)
    for k in range(rows):
        text = sown[k]
        limit = counts[text] - (k - start[text])
        ok = jnp.where((lane4 == text) & (lower < limit), clip_bound, 0.0)
        bnd[k] = jnp.broadcast_to(jnp.max(ok, axis=1, keepdims=True), (pos, LANES))

    tiles = max(c for c in range(1, 9) if (win - 1) % c == 0)

    def partial_sums(j, store):
        base = first_tile(j)
        for t in range(texts):
            here[t] = pubs[j, t].astype(f32)

        def some(count, source, at, to):
            acc = [jnp.zeros((pos, LANES), f32)] * count
            for c in range(count):
                pref[0, :, c * LANES:(c + 1) * LANES] = acc[c]
            for k in range(rows):
                row = order[k]
                text = sown[k]
                b = bnd[k]
                for c in range(count):
                    p = source[row, :, pl.ds(pl.multiple_of(at + c * LANES, LANES), LANES)].astype(f32)
                    u = here[text, :, pl.ds(pl.multiple_of(to + c * LANES, LANES), LANES)]
                    acc[c] = acc[c] + jnp.minimum(jnp.maximum(p - u, -b), b)
                    pref[k + 1, :, c * LANES:(c + 1) * LANES] = acc[c]
            for t in range(texts):
                v = pref[start[t + 1], :, :count * LANES] - pref[start[t], :, :count * LANES]
                store(t, pl.ds(pl.multiple_of(to, LANES), count * LANES), v)

        def chunk(i, c):
            to = i * (tiles * LANES)
            some(tiles, pv, base * LANES + to, to)
            return c

        lax.fori_loop(0, (win - 1) // tiles, chunk, 0)
        some(1, xt, j * LANES, (win - 1) * LANES)

    def coded(v, scale):
        return jnp.round(v * scale).astype(jnp.int32).astype(jnp.int16)

    def decoded(q, scale):
        return q.astype(jnp.int32).astype(f32) * (1.0 / scale)

    def column(i):
        return lax.rem(z - i + half, half)

    def step(i, c):
        @pl.when(i < half)
        def _():
            zi = column(i)
            j = 2 * zi + x

            @pl.when(i > 0)
            def _():
                remote(pubs.at[j], pubs.at[j], ag_f.at[zi], ag_r.at[j], {"ref": partner}).wait_recv()
                remote(pubs.at[j], pubs.at[j], ag_f.at[zi], ag_r.at[j], {"ref": partner}).start()

            def store(t, lanes, v):
                keep[zi, t, :, lanes] = v

            partial_sums(j, store)

        @pl.when((i >= 1) & (i <= half))
        def _():
            zi = column(i - 1)
            j = 2 * zi + 1 - x
            remote(pubs.at[j], pubs.at[j], ag_f.at[zi], ag_r.at[j], {"ref": partner}).wait_recv()

            def store(t, lanes, v):
                snd1[zi, t, :, lanes] = coded(v, scale1)

            partial_sums(j, store)
            remote(snd1.at[zi], rs1.at[zi], rs1_s.at[zi], rs1_r.at[zi], {"ref": partner}).start()

        @pl.when(i >= 2)
        def _():
            zi = column(i - 2)
            remote(snd1.at[zi], rs1.at[zi], rs1_s.at[zi], rs1_r.at[zi], {"ref": partner}).wait_recv()

            @pl.when(i == 2)
            def _():
                for t in range(texts):
                    keep[zi, t] = keep[zi, t] + decoded(rs1[zi, t], scale1)

            @pl.when(i > 2)
            def _():
                for t in range(texts):
                    snd2[zi, t] = coded(keep[zi, t] + decoded(rs1[zi, t], scale1), scale2)
                remote(snd2.at[zi], rs2.at[z], rs2_s.at[zi], rs2_r.at[z], {"ref": 2 * zi + x}).start()

        return c

    lax.fori_loop(0, half + 2, step, 0)

    def gather(k, c):
        zi = lax.rem(z + k, half)
        remote(snd2.at[zi], rs2.at[zi], rs2_s.at[zi], rs2_r.at[zi], {"ref": 2 * zi + x}).wait_recv()
        for t in range(texts):
            keep[z, t] = keep[z, t] + decoded(rs2[zi, t], scale2)
        return c

    lax.fori_loop(1, half, gather, 0)

    first_column = (mv * n + me) * piece
    at_column = lax.broadcasted_iota(jnp.int32, (pos, piece), 1) + first_column
    at_pos = lax.broadcasted_iota(jnp.int32, (pos, 1), 0)
    lse_all = jnp.zeros((pos, LANES), f32)
    picked_all = jnp.zeros((pos, LANES), f32)
    for t in range(texts):
        summed = pltpu.roll(keep[z, t], lax.rem(wl - shift, wl), 1)[:, :piece]
        root = jnp.sqrt(jnp.full((pos, LANES), counts[t].astype(f32), f32))
        factor = (1.0 / (clip_bound * root))[:, :1]
        combined = pub[t].astype(f32) + summed * factor + noise[t].astype(f32)
        combined_out[t] = combined
        peak = jnp.max(combined, axis=1, keepdims=True)
        total = jnp.sum(jnp.exp(combined - peak), axis=1, keepdims=True)
        token = jnp.zeros((pos, 1), jnp.int32)
        for p in range(pos):
            token = jnp.where(at_pos == p, tokens[t, p], token)
        picked = jnp.sum(jnp.where(at_column == token, combined, 0.0), axis=1, keepdims=True)
        lse_all = jnp.where(lane4 == t, peak + jnp.log(total), lse_all)
        picked_all = jnp.where(lane4 == t, picked, picked_all)

    def exchange(slots, send, recv, index, count, axis, lse, picked):
        slots[index, :pos] = lse
        slots[index, pos:2 * pos] = picked

        def send_one(k, c):
            remote(slots.at[index], slots.at[index], send, recv, {axis: lax.rem(index + k, count)}).start()
            return c

        lax.fori_loop(1, count, send_one, 0)
        others = slots.at[pl.ds(0, count - 1)]
        pltpu.make_async_copy(others, others, recv).wait()
        pltpu.make_async_copy(others, others, send).wait()
        top = lax.fori_loop(1, count, lambda j, a: jnp.maximum(a, slots[j, :pos]), slots[0, :pos])
        zero = jnp.zeros((pos, LANES), f32)
        total, found = lax.fori_loop(
            0, count,
            lambda j, a: (a[0] + jnp.exp(slots[j, :pos] - top), a[1] + slots[j, pos:2 * pos]),
            (zero, zero),
        )
        return top + jnp.log(total), found

    lse, picked = exchange(st1, st1_s, st1_r, mv, nv, "voc", lse_all, picked_all)
    lse, picked = exchange(st2, st2_s, st2_r, me, n, "ref", lse, picked)
    stats_out[0] = lse
    stats_out[1] = picked

    def sent(i, c):
        remote(pubs.at[me], pubs.at[me], ag_s.at[i], ag_r.at[me], {"ref": partner}).wait_send()
        remote(snd1.at[i], rs1.at[i], rs1_s.at[i], rs1_r.at[i], {"ref": partner}).wait_send()

        @pl.when(i != z)
        def _():
            remote(pubs.at[me], pubs.at[me], ag_f.at[i], ag_r.at[me], {"ref": partner}).wait_send()
            remote(snd2.at[i], rs2.at[i], rs2_s.at[i], rs2_r.at[i], {"ref": partner}).wait_send()

        return c

    lax.fori_loop(0, half, sent, 0)


def body(n, nv, private_logits, public_logits, noise, owner, counts, tokens):
    rows, pos, width = private_logits.shape
    texts, _, piece = public_logits.shape
    half = n // 2
    full = width // LANES
    win = max(-(-((j * piece) % LANES + piece) // LANES) for j in range(n))
    while min(j * piece - LANES * min(j * piece // LANES, full + 1 - win) for j in range(n)) < 0:
        win += 1
    wl = win * LANES
    bf16, f32, i16 = jnp.bfloat16, jnp.float32, jnp.int16
    smem = pl.BlockSpec(memory_space=pltpu.SMEM)
    vmem = pl.BlockSpec(memory_space=pltpu.VMEM)
    dma = pltpu.SemaphoreType.DMA
    combined, stats = pl.pallas_call(
        functools.partial(kernel, n, nv, rows, texts, pos, width, piece, win),
        out_shape=(
            jax.ShapeDtypeStruct((texts, pos, piece), f32),
            jax.ShapeDtypeStruct((2, pos, LANES), f32),
        ),
        in_specs=[smem, smem, smem, pl.BlockSpec(memory_space=pl.ANY), vmem, vmem],
        out_specs=(vmem, vmem),
        scratch_shapes=[
            pltpu.VMEM((rows, pos, width), bf16),
            pltpu.VMEM((rows, pos, n * LANES), bf16),
            pltpu.VMEM((texts, pos, wl), f32),
            pltpu.VMEM((n, texts, pos, wl), bf16),
            pltpu.VMEM((texts, pos, wl), f32),
            pltpu.VMEM((rows + 1, pos, 8 * LANES), f32),
            pltpu.VMEM((half, texts, pos, wl), f32),
            pltpu.VMEM((half, texts, pos, wl), i16),
            pltpu.VMEM((half, texts, pos, wl), i16),
            pltpu.VMEM((half, texts, pos, wl), i16),
            pltpu.VMEM((half, texts, pos, wl), i16),
            pltpu.VMEM((n, 8, LANES), jnp.int32),
            pltpu.VMEM((nv, 2 * pos, LANES), f32),
            pltpu.VMEM((n, 2 * pos, LANES), f32),
            pltpu.VMEM((rows, pos, LANES), f32),
            pltpu.SMEM((rows,), jnp.int32),
            pltpu.SMEM((rows,), jnp.int32),
            pltpu.SMEM((texts + 1,), jnp.int32),
            dma, dma, dma,
            dma((half,)), dma((half,)), dma((n,)),
            dma((half,)), dma((half,)), dma((half,)), dma((half,)),
            dma, dma, dma, dma,
        ],
        compiler_params=pltpu.CompilerParams(
            collective_id=0, has_side_effects=True, vmem_limit_bytes=56 * 1024 * 1024
        ),
        cost_estimate=pl.CostEstimate(
            flops=6 * rows * pos * width, bytes_accessed=2 * rows * pos * width, transcendentals=0
        ),
        name="private_scores",
    )(owner, counts, tokens, private_logits, public_logits, noise)
    lse = stats[0, :, :texts].T
    logprobs = combined - lse[:, :, None]
    target = stats[1, :, :texts].T - lse
    return (logprobs, target)


def solution(mesh):
    return jax.shard_map(
        functools.partial(body, mesh.shape["ref"], mesh.shape["voc"]),
        mesh=mesh,
        in_specs=(
            P("ref", None, "voc"),
            P(None, None, ("voc", "ref")),
            P(None, None, ("voc", "ref")),
            P("ref"),
            P(),
            P(),
        ),
        out_specs=(P(None, None, ("voc", "ref")), P()),
        check_vma=False,
    )
```

time: 891 us -> 55.9 us (0.06)
  blocking collectives: 711 us -> 0 us
  waiting for transfers between devices: 98.9 us -> 0 us
  Pallas kernels: 0 us -> 51.2 us
  local copies, waits for them, and re-layouts: 50 us -> 1.43 us
  between operations: 15.5 us -> 0.64 us
  matrix products: 10.9 us -> 0 us
    all_gather x1 -> x0, blocking collectives: 622 us -> none  [body(): lax.all_gather(public_logits, 'ref', axis=2, tiled=True).astype(jnp.float32)]
    unnamed x2 -> x0, waiting for transfers between devices: 98.9 us -> none
    pallas_call x0 -> x1, Pallas kernels: none -> 51.2 us  [body(): pl.pallas_call(functools.partial(kernel, n, nv, rows, texts, pos, width,...]
    all_gather x2 -> x0, local copies, waits for them, and re-layouts: 41.8 us -> none  [the longest x1 41.7 us: body(): lax.all_gather(public_logits, 'ref', axis=2, tiled=True).astype(jnp.float32)]
    pmax x1 -> x0, blocking collectives: 40.1 us -> none  [wide_stats(): row_peak = lax.pmax(jnp.max(combined, axis=2), ('ref', 'voc'))]
    psum x1 -> x0, blocking collectives: 39 us -> none  [wide_stats(): lax.psum((jnp.sum(jnp.exp(combined - row_peak[:, :, None]), axis=2), pick...]
    dot_general x2 -> x0, matrix products: 10.9 us -> none  [the longest x1 5.74 us: body(): jnp.einsum('rt,tpv->rpv', select, lax.all_gather(public_logits, 'ref', ax...]
    unnamed x1 -> x0, blocking collectives: 10.6 us -> none
  transfers between devices with their start and end apart: 1 -> 0, of which waited for: 1 -> 0; matrix products, arithmetic and copies ran while one was open for 0% -> 0% of each run, Pallas kernels for 0% -> 0%
where the time goes in v1:
time: 55.9 us; the launch traced here: 55.7 us
  Pallas kernels  51.2 us (92%)
  other arithmetic  2.45 us (4%)
  local copies, waits for them, and re-layouts  1.43 us (3%)
  between operations  0.64 us (1%)
    pallas_call x1, Pallas kernels, body(): pl.pallas_call(functools.partial(kernel, n, nv, rows, texts, pos, width,...  51.2 us
    sub x1, other arithmetic, body(): logprobs = combined - lse[:, :, None]  1.76 us

profile of v1, /device:TPU:0, one launch (start us, length us, event | category | flops | bytes accessed | tf_op | source)
XLA Modules:
  0.0 55.7 jit_solution(7973671372789895012)
XLA Ops:
  0.6 51.2 %private_scores.1 = (f32[4,4,4008]{2,1,0:T(4,128)}, f32[2,4,128]{2,1,0:T(4,128)}) custom-call(s32[12]{0:T(128)} %owner.1, s32[4]{0:T(128)} %counts.1, s32[4,4]{1,0:T(4,128)} %tokens.1, bf16[12,4,32064]{2,1,0:T(4,128)(2,1)} %priv.1, bf16[4,4,4008]{2,1,0:T(4,128)(2,1)} %pub.1, bf16[4,4,4008]{2,1,0:T(4,128)(2,1)} %noise.1), custom_call_target="tpu_custom_call" | custom-call | flops 9234432 | bytes 3078144 | tf_op jit(solution)/shard_map/private_scores/pallas_call | solution.py:313
  51.8 0.7 %bitcast_subtract_fusion = f32[4,4]{0,1:T(4,128)S(1)} fusion(f32[2,4,128]{2,1,0:T(4,128)} %get-tuple-element.5), kind=kLoop, calls=%fused_computation.1 | loop fusion | flops 16 | bytes 192 | tf_op jit(solution)/shard_map/sub | solution.py:355
  52.5 0.7 %slice_bitcast_fusion = f32[4,4]{0,1:T(4,128)S(1)} fusion(f32[2,4,128]{2,1,0:T(4,128)} %get-tuple-element.5), kind=kLoop, calls=%fused_computation.2 | loop fusion | bytes 128 | tf_op jit(solution)/shard_map/transpose | solution.py:353
  53.2 0.1 copy.8
  53.3 1.8 %broadcast_subtract_fusion = f32[4,4,4008]{2,1,0:T(4,128)} fusion(f32[4,4,4008]{2,1,0:T(4,128)} %get-tuple-element.4, f32[4,4]{1,0:T(4,128)S(1)} %copy.8), kind=kLoop, calls=%fused_computation | loop fusion | flops 64128 | bytes 513088 | tf_op jit(solution)/shard_map/sub | solution.py:354
  55.0 0.7 %copy.9 = f32[4,4]{1,0:T(4,128)} copy(f32[4,4]{0,1:T(4,128)S(1)} %bitcast_subtract_fusion) | data formatting | bytes 128

commit v2 on v1

--- a/solution.py
+++ b/solution.py
@@ -73,6 +73,28 @@
 
     own = [owner[r] for r in range(rows)]
     hits = [sum((o == t).astype(jnp.int32) for o in own) for t in range(texts)]
+    lane8 = lax.broadcasted_iota(jnp.int32, (8, LANES), 1)
+    mine = jnp.zeros((8, LANES), jnp.int32)
+    for t in range(texts):
+        mine = jnp.where(lane8 == t, hits[t], mine)
+    hist[me] = mine
+
+    pl.semaphore_wait(barrier, n - 1 + nv - 1)
+
+    def send_hist(k, c):
+        remote(hist.at[me], hist.at[me], hist_s, hist_r, {"ref": lax.rem(me + k, n)}).start()
+        return c
+
+    lax.fori_loop(1, n, send_hist, 0)
+    remote(pubs.at[me], pubs.at[me], ag_s.at[0], ag_r.at[me], {"ref": partner}).start()
+
+    def send_own(k, c):
+        peer = 2 * lax.rem(z + k, half) + x
+        remote(pubs.at[me], pubs.at[me], ag_s.at[k], ag_r.at[me], {"ref": peer}).start()
+        return c
+
+    lax.fori_loop(1, half, send_own, 0)
+
     begin = [jnp.int32(0)]
     for t in range(texts):
         begin.append(begin[-1] + hits[t])
@@ -94,28 +116,6 @@
         order[k] = at
         sown[k] = sum((begin[t] <= k).astype(jnp.int32) for t in range(1, texts))
 
-    lane8 = lax.broadcasted_iota(jnp.int32, (8, LANES), 1)
-    mine = jnp.zeros((8, LANES), jnp.int32)
-    for t in range(texts):
-        mine = jnp.where(lane8 == t, hits[t], mine)
-    hist[me] = mine
-
-    pl.semaphore_wait(barrier, n - 1 + nv - 1)
-
-    def send_hist(k, c):
-        remote(hist.at[me], hist.at[me], hist_s, hist_r, {"ref": lax.rem(me + k, n)}).start()
-        return c
-
-    lax.fori_loop(1, n, send_hist, 0)
-    remote(pubs.at[me], pubs.at[me], ag_s.at[0], ag_r.at[me], {"ref": partner}).start()
-
-    def send_own(k, c):
-        peer = 2 * lax.rem(z + k, half) + x
-        remote(pubs.at[me], pubs.at[me], ag_s.at[k], ag_r.at[me], {"ref": peer}).start()
-        return c
-
-    lax.fori_loop(1, half, send_own, 0)
-
     load.wait()
     for j in range(n):
         s = min(j * piece // LANES, full + 1 - win) + win - 1
@@ -295,6 +295,17 @@
         return c
 
     lax.fori_loop(0, half, sent, 0)
+
+
+def finish(texts, pos, combined, stats, logprobs, target):
+    lse = stats[0]
+    score = stats[1] - lse
+    at_pos = lax.broadcasted_iota(jnp.int32, (pos, pos), 0)
+    at_lane = lax.broadcasted_iota(jnp.int32, (pos, pos), 1)
+    for t in range(texts):
+        logprobs[t] = combined[t] - lse[:, t:t + 1]
+        column = jnp.where(at_pos == at_lane, score[:, t:t + 1], 0.0)
+        target[t:t + 1, :] = jnp.sum(column, axis=0, keepdims=True)
 
 
 def body(n, nv, private_logits, public_logits, noise, owner, counts, tokens):
@@ -350,10 +361,16 @@
         ),
         name="private_scores",
     )(owner, counts, tokens, private_logits, public_logits, noise)
-    lse = stats[0, :, :texts].T
-    logprobs = combined - lse[:, :, None]
-    target = stats[1, :, :texts].T - lse
-    return (logprobs, target)
+    return pl.pallas_call(
+        functools.partial(finish, texts, pos),
+        out_shape=(
+            jax.ShapeDtypeStruct((texts, pos, piece), f32),
+            jax.ShapeDtypeStruct((texts, pos), f32),
+        ),
+        in_specs=[vmem, vmem],
+        out_specs=(vmem, vmem),
+        name="subtract_lse",
+    )(combined, stats)
 
 
 def solution(mesh):

time: 55.9 us -> 53.7 us (0.961)
  other arithmetic: 2.45 us -> 0 us
  Pallas kernels: 51.2 us -> 52.9 us
  local copies, waits for them, and re-layouts: 1.43 us -> 0 us
    sub x2 -> x0, other arithmetic: 2.45 us -> none  [the longest x1 1.76 us: body(): logprobs = combined - lse[:, :, None]]
    pallas_call x0 -> x1, Pallas kernels: none -> 1.75 us  [body(): pl.pallas_call(functools.partial(finish, texts, pos), out_shape=(jax.Shap...]
    transpose x2 -> x0, local copies, waits for them, and re-layouts: 0.77 us -> none  [body(): lse = stats[0, :, :texts].T]
    unnamed x1 -> x0, local copies, waits for them, and re-layouts: 0.66 us -> none
where the time goes in v2:
time: 53.7 us; the launch traced here: 53.5 us
  Pallas kernels  52.9 us (99%)
  between operations  0.64 us (1%)
    pallas_call x1, Pallas kernels, body(): pl.pallas_call(functools.partial(kernel, n, nv, rows, texts, pos, width,...  51.2 us
    pallas_call x1, Pallas kernels, body(): pl.pallas_call(functools.partial(finish, texts, pos), out_shape=(jax.Shap...  1.75 us

profile of v2, /device:TPU:0, one launch (start us, length us, event | category | flops | bytes accessed | tf_op | source)
XLA Modules:
  0.0 53.5 jit_solution(2624799127723026381)
XLA Ops:
  0.6 51.2 %private_scores.1 = (f32[4,4,4008]{2,1,0:T(4,128)}, f32[2,4,128]{2,1,0:T(4,128)}) custom-call(s32[12]{0:T(128)} %owner.1, s32[4]{0:T(128)} %counts.1, s32[4,4]{1,0:T(4,128)} %tokens.1, bf16[12,4,32064]{2,1,0:T(4,128)(2,1)} %priv.1, bf16[4,4,4008]{2,1,0:T(4,128)(2,1)} %pub.1, bf16[4,4,4008]{2,1,0:T(4,128)(2,1)} %noise.1), custom_call_target="tpu_custom_call" | custom-call | flops 9234432 | bytes 3078144 | tf_op jit(solution)/shard_map/private_scores/pallas_call | solution.py:324
  51.8 1.8 %subtract_lse.1 = (f32[4,4,4008]{2,1,0:T(4,128)}, f32[4,4]{1,0:T(4,128)}) custom-call(f32[4,4,4008]{2,1,0:T(4,128)} %get-tuple-element.4.combined, f32[2,4,128]{2,1,0:T(4,128)} %get-tuple-element.5.stats), custom_call_target="tpu_custom_call" | custom-call | tf_op jit(solution)/shard_map/subtract_lse/pallas_call | solution.py:364

commit v3 on v2

--- a/solution.py
+++ b/solution.py
@@ -25,7 +25,7 @@
     combined_out, stats_out,
     pv, xt, pubf, pubs, here, pref, keep, snd1, rs1, snd2, rs2,
     hist, st1, st2, bnd, order, sown, start,
-    priv_sem, hist_s, hist_r, ag_s, ag_f, ag_r, rs1_s, rs1_r, rs2_s, rs2_r,
+    priv_sem, hist_s, hist_r, ag_x, ag_up, ag_dn, ag_r, rs1_s, rs1_r, rs2_s, rs2_r,
     st1_s, st1_r, st2_s, st2_r,
 ):
     f32 = jnp.float32
@@ -81,20 +81,25 @@
 
     pl.semaphore_wait(barrier, n - 1 + nv - 1)
 
+    def pass_on(zi):
+        j = 2 * zi + x
+        remote(pubs.at[j], pubs.at[j], ag_x.at[zi], ag_r.at[j], {"ref": partner}).start()
+
+        @pl.when((zi <= z) & (z < half - 1))
+        def _():
+            remote(pubs.at[j], pubs.at[j], ag_up.at[zi], ag_r.at[j], {"ref": me + 2}).start()
+
+        @pl.when((zi >= z) & (z > 0))
+        def _():
+            remote(pubs.at[j], pubs.at[j], ag_dn.at[zi], ag_r.at[j], {"ref": me - 2}).start()
+
+    pass_on(z)
+
     def send_hist(k, c):
         remote(hist.at[me], hist.at[me], hist_s, hist_r, {"ref": lax.rem(me + k, n)}).start()
         return c
 
     lax.fori_loop(1, n, send_hist, 0)
-    remote(pubs.at[me], pubs.at[me], ag_s.at[0], ag_r.at[me], {"ref": partner}).start()
-
-    def send_own(k, c):
-        peer = 2 * lax.rem(z + k, half) + x
-        remote(pubs.at[me], pubs.at[me], ag_s.at[k], ag_r.at[me], {"ref": peer}).start()
-        return c
-
-    lax.fori_loop(1, half, send_own, 0)
-
     begin = [jnp.int32(0)]
     for t in range(texts):
         begin.append(begin[-1] + hits[t])
@@ -177,56 +182,67 @@
     def decoded(q, scale):
         return q.astype(jnp.int32).astype(f32) * (1.0 / scale)
 
+    nearer = jnp.minimum(z, half - 1 - z)
+
     def column(i):
-        return lax.rem(z - i + half, half)
-
-    def step(i, c):
+        side = jnp.where(lax.rem(i, 2) == 1, -lax.div(i + 1, 2), lax.div(i, 2))
+        rest = jnp.where(z < half - 1 - z, i, half - 1 - i)
+        return jnp.where(i <= 2 * nearer, z + side, rest)
+
+    def own_column(i):
+        zi = column(i)
+
+        def store(t, lanes, v):
+            keep[zi, t, :, lanes] = v
+
+        partial_sums(2 * zi + x, store)
+
+    def arrive(i, c):
+        zi = column(i)
+        j = 2 * zi + x
+        remote(pubs.at[j], pubs.at[j], ag_x.at[zi], ag_r.at[j], {"ref": partner}).wait_recv()
+        pass_on(zi)
+
+        @pl.when(i >= 2)
+        def _():
+            own_column(i - 1)
+
+        return c
+
+    def other_column(i, c):
+        zi = column(lax.rem(i, half))
+        j = 2 * zi + 1 - x
+        remote(pubs.at[j], pubs.at[j], ag_x.at[zi], ag_r.at[j], {"ref": partner}).wait_recv()
+
+        def store(t, lanes, v):
+            snd1[zi, t, :, lanes] = coded(v, scale1)
+
+        partial_sums(j, store)
+        remote(snd1.at[zi], rs1.at[zi], rs1_s.at[zi], rs1_r.at[zi], {"ref": partner}).start()
+        return c
+
+    def add_partner(i, c):
+        zi = column(lax.rem(i, half))
+        remote(snd1.at[zi], rs1.at[zi], rs1_s.at[zi], rs1_r.at[zi], {"ref": partner}).wait_recv()
+
+        @pl.when(i == half)
+        def _():
+            for t in range(texts):
+                keep[zi, t] = keep[zi, t] + decoded(rs1[zi, t], scale1)
+
         @pl.when(i < half)
         def _():
-            zi = column(i)
-            j = 2 * zi + x
-
-            @pl.when(i > 0)
-            def _():
-                remote(pubs.at[j], pubs.at[j], ag_f.at[zi], ag_r.at[j], {"ref": partner}).wait_recv()
-                remote(pubs.at[j], pubs.at[j], ag_f.at[zi], ag_r.at[j], {"ref": partner}).start()
-
-            def store(t, lanes, v):
-                keep[zi, t, :, lanes] = v
-
-            partial_sums(j, store)
-
-        @pl.when((i >= 1) & (i <= half))
-        def _():
-            zi = column(i - 1)
-            j = 2 * zi + 1 - x
-            remote(pubs.at[j], pubs.at[j], ag_f.at[zi], ag_r.at[j], {"ref": partner}).wait_recv()
-
-            def store(t, lanes, v):
-                snd1[zi, t, :, lanes] = coded(v, scale1)
-
-            partial_sums(j, store)
-            remote(snd1.at[zi], rs1.at[zi], rs1_s.at[zi], rs1_r.at[zi], {"ref": partner}).start()
-
-        @pl.when(i >= 2)
-        def _():
-            zi = column(i - 2)
-            remote(snd1.at[zi], rs1.at[zi], rs1_s.at[zi], rs1_r.at[zi], {"ref": partner}).wait_recv()
-
-            @pl.when(i == 2)
-            def _():
-                for t in range(texts):
-                    keep[zi, t] = keep[zi, t] + decoded(rs1[zi, t], scale1)
-
-            @pl.when(i > 2)
-            def _():
-                for t in range(texts):
-                    snd2[zi, t] = coded(keep[zi, t] + decoded(rs1[zi, t], scale1), scale2)
-                remote(snd2.at[zi], rs2.at[z], rs2_s.at[zi], rs2_r.at[z], {"ref": 2 * zi + x}).start()
-
-        return c
-
-    lax.fori_loop(0, half + 2, step, 0)
+            for t in range(texts):
+                snd2[zi, t] = coded(keep[zi, t] + decoded(rs1[zi, t], scale1), scale2)
+            remote(snd2.at[zi], rs2.at[z], rs2_s.at[zi], rs2_r.at[z], {"ref": 2 * zi + x}).start()
+
+        return c
+
+    own_column(jnp.int32(0))
+    lax.fori_loop(1, half, arrive, 0)
+    lax.fori_loop(1, half + 1, other_column, 0)
+    own_column(jnp.int32(half - 1))
+    lax.fori_loop(1, half + 1, add_partner, 0)
 
     def gather(k, c):
         zi = lax.rem(z + k, half)
@@ -284,12 +300,19 @@
     stats_out[1] = picked
 
     def sent(i, c):
-        remote(pubs.at[me], pubs.at[me], ag_s.at[i], ag_r.at[me], {"ref": partner}).wait_send()
+        remote(pubs.at[me], pubs.at[me], ag_x.at[i], ag_r.at[me], {"ref": partner}).wait_send()
         remote(snd1.at[i], rs1.at[i], rs1_s.at[i], rs1_r.at[i], {"ref": partner}).wait_send()
 
+        @pl.when((i <= z) & (z < half - 1))
+        def _():
+            remote(pubs.at[me], pubs.at[me], ag_up.at[i], ag_r.at[me], {"ref": partner}).wait_send()
+
+        @pl.when((i >= z) & (z > 0))
+        def _():
+            remote(pubs.at[me], pubs.at[me], ag_dn.at[i], ag_r.at[me], {"ref": partner}).wait_send()
+
         @pl.when(i != z)
         def _():
-            remote(pubs.at[me], pubs.at[me], ag_f.at[i], ag_r.at[me], {"ref": partner}).wait_send()
             remote(snd2.at[i], rs2.at[i], rs2_s.at[i], rs2_r.at[i], {"ref": partner}).wait_send()
 
         return c
@@ -349,7 +372,7 @@
             pltpu.SMEM((rows,), jnp.int32),
             pltpu.SMEM((texts + 1,), jnp.int32),
             dma, dma, dma,
-            dma((half,)), dma((half,)), dma((n,)),
+            dma((half,)), dma((half,)), dma((half,)), dma((n,)),
             dma((half,)), dma((half,)), dma((half,)), dma((half,)),
             dma, dma, dma, dma,
         ],

time: 53.7 us -> 52.1 us (0.970)
  Pallas kernels: 52.9 us -> 51.4 us
    pallas_call x1, Pallas kernels: 51.2 us -> 49.6 us  [body(): pl.pallas_call(functools.partial(kernel, n, nv, rows, texts, pos, width,...]
where the time goes in v3:
time: 52.1 us; the launch traced here: 52 us
  Pallas kernels  51.4 us (99%)
  between operations  0.64 us (1%)
    pallas_call x1, Pallas kernels, body(): pl.pallas_call(functools.partial(kernel, n, nv, rows, texts, pos, width,...  49.6 us
    pallas_call x1, Pallas kernels, body(): pl.pallas_call(functools.partial(finish, texts, pos), out_shape=(jax.Shap...  1.75 us

profile of v3, /device:TPU:0, one launch (start us, length us, event | category | flops | bytes accessed | tf_op | source)
XLA Modules:
  0.0 52.0 jit_solution(7320705280919292756)
XLA Ops:
  0.6 49.6 %private_scores.1 = (f32[4,4,4008]{2,1,0:T(4,128)}, f32[2,4,128]{2,1,0:T(4,128)}) custom-call(s32[12]{0:T(128)} %owner.1, s32[4]{0:T(128)} %counts.1, s32[4,4]{1,0:T(4,128)} %tokens.1, bf16[12,4,32064]{2,1,0:T(4,128)(2,1)} %priv.1, bf16[4,4,4008]{2,1,0:T(4,128)(2,1)} %pub.1, bf16[4,4,4008]{2,1,0:T(4,128)(2,1)} %noise.1), custom_call_target="tpu_custom_call" | custom-call | flops 9234432 | bytes 3078144 | tf_op jit(solution)/shard_map/private_scores/pallas_call | solution.py:347
  50.2 1.8 %subtract_lse.1 = (f32[4,4,4008]{2,1,0:T(4,128)}, f32[4,4]{1,0:T(4,128)}) custom-call(f32[4,4,4008]{2,1,0:T(4,128)} %get-tuple-element.4.combined, f32[2,4,128]{2,1,0:T(4,128)} %get-tuple-element.5.stats), custom_call_target="tpu_custom_call" | custom-call | tf_op jit(solution)/shard_map/subtract_lse/pallas_call | solution.py:387

commit v4 on v3

--- a/solution.py
+++ b/solution.py
@@ -32,6 +32,8 @@
     half = n // 2
     full = width // LANES
     wl = win * LANES
+    pairs = win // 2
+    hl = pairs * LANES
     me = lax.axis_index("ref")
     mv = lax.axis_index("voc")
     z = lax.div(me, 2)
@@ -69,12 +71,13 @@
     for t in range(texts):
         pubf[t, :, :piece] = pub[t].astype(f32)
     for t in range(texts):
-        pubs[me, t] = pltpu.roll(pubf[t], shift, 1).astype(jnp.bfloat16)
+        moved = pltpu.roll(pubf[t], shift, 1)
+        pubs[me, t] = jnp.concatenate([moved[:, :hl], moved[:, hl:]], axis=0).astype(jnp.bfloat16)
 
     own = [owner[r] for r in range(rows)]
     hits = [sum((o == t).astype(jnp.int32) for o in own) for t in range(texts)]
-    lane8 = lax.broadcasted_iota(jnp.int32, (8, LANES), 1)
-    mine = jnp.zeros((8, LANES), jnp.int32)
+    lane8 = lax.broadcasted_iota(jnp.int32, (2 * pos, LANES), 1)
+    mine = jnp.zeros((2 * pos, LANES), jnp.int32)
     for t in range(texts):
         mine = jnp.where(lane8 == t, hits[t], mine)
     hist[me] = mine
@@ -93,13 +96,13 @@
         def _():
             remote(pubs.at[j], pubs.at[j], ag_dn.at[zi], ag_r.at[j], {"ref": me - 2}).start()
 
-    pass_on(z)
-
     def send_hist(k, c):
         remote(hist.at[me], hist.at[me], hist_s, hist_r, {"ref": lax.rem(me + k, n)}).start()
         return c
 
     lax.fori_loop(1, n, send_hist, 0)
+    pass_on(z)
+
     begin = [jnp.int32(0)]
     for t in range(texts):
         begin.append(begin[-1] + hits[t])
@@ -134,47 +137,37 @@
     got = hist.at[pl.ds(0, n - 1)]
     pltpu.make_async_copy(got, got, hist_r).wait()
     pltpu.make_async_copy(got, got, hist_s).wait()
-    lower = jnp.zeros((8, LANES), jnp.int32)
+    lower = jnp.zeros((2 * pos, LANES), jnp.int32)
     lower = lax.fori_loop(0, n, lambda j, a: a + jnp.where(j < me, hist[j], 0), lower)
-    lower = lower[:pos]
-    lane4 = lax.broadcasted_iota(jnp.int32, (pos, LANES), 1)
+    lane4 = lane8[:pos]
+    pref[0] = jnp.zeros_like(pref[0])
     for k in range(rows):
         text = sown[k]
         limit = counts[text] - (k - start[text])
-        ok = jnp.where((lane4 == text) & (lower < limit), clip_bound, 0.0)
-        bnd[k] = jnp.broadcast_to(jnp.max(ok, axis=1, keepdims=True), (pos, LANES))
-
-    tiles = max(c for c in range(1, 9) if (win - 1) % c == 0)
+        ok = jnp.where((lane8 == text) & (lower < limit), clip_bound, 0.0)
+        bnd[k] = jnp.broadcast_to(jnp.max(ok, axis=1, keepdims=True), (2 * pos, LANES))
 
     def partial_sums(j, store):
-        base = first_tile(j)
+        base = first_tile(j) * LANES
         for t in range(texts):
             here[t] = pubs[j, t].astype(f32)
-
-        def some(count, source, at, to):
-            acc = [jnp.zeros((pos, LANES), f32)] * count
-            for c in range(count):
-                pref[0, :, c * LANES:(c + 1) * LANES] = acc[c]
-            for k in range(rows):
-                row = order[k]
-                text = sown[k]
-                b = bnd[k]
-                for c in range(count):
-                    p = source[row, :, pl.ds(pl.multiple_of(at + c * LANES, LANES), LANES)].astype(f32)
-                    u = here[text, :, pl.ds(pl.multiple_of(to + c * LANES, LANES), LANES)]
-                    acc[c] = acc[c] + jnp.minimum(jnp.maximum(p - u, -b), b)
-                    pref[k + 1, :, c * LANES:(c + 1) * LANES] = acc[c]
-            for t in range(texts):
-                v = pref[start[t + 1], :, :count * LANES] - pref[start[t], :, :count * LANES]
-                store(t, pl.ds(pl.multiple_of(to, LANES), count * LANES), v)
-
-        def chunk(i, c):
-            to = i * (tiles * LANES)
-            some(tiles, pv, base * LANES + to, to)
-            return c
-
-        lax.fori_loop(0, (win - 1) // tiles, chunk, 0)
-        some(1, xt, j * LANES, (win - 1) * LANES)
+        acc = [jnp.zeros((2 * pos, LANES), f32)] * pairs
+        for k in range(rows):
+            row = order[k]
+            text = sown[k]
+            b = bnd[k]
+            for c in range(pairs):
+                low = pv[row, :, pl.ds(pl.multiple_of(base + c * LANES, LANES), LANES)]
+                if c < pairs - 1:
+                    high = pv[row, :, pl.ds(pl.multiple_of(base + hl + c * LANES, LANES), LANES)]
+                else:
+                    high = xt[row, :, pl.ds(pl.multiple_of(j * LANES, LANES), LANES)]
+                p = jnp.concatenate([low.astype(f32), high.astype(f32)], axis=0)
+                u = here[text, :, c * LANES:(c + 1) * LANES]
+                acc[c] = acc[c] + jnp.minimum(jnp.maximum(p - u, -b), b)
+                pref[k + 1, :, c * LANES:(c + 1) * LANES] = acc[c]
+        for t in range(texts):
+            store(t, pref[start[t + 1]] - pref[start[t]])
 
     def coded(v, scale):
         return jnp.round(v * scale).astype(jnp.int32).astype(jnp.int16)
@@ -192,8 +185,8 @@
     def own_column(i):
         zi = column(i)
 
-        def store(t, lanes, v):
-            keep[zi, t, :, lanes] = v
+        def store(t, v):
+            keep[zi, t] = v
 
         partial_sums(2 * zi + x, store)
 
@@ -214,8 +207,8 @@
         j = 2 * zi + 1 - x
         remote(pubs.at[j], pubs.at[j], ag_x.at[zi], ag_r.at[j], {"ref": partner}).wait_recv()
 
-        def store(t, lanes, v):
-            snd1[zi, t, :, lanes] = coded(v, scale1)
+        def store(t, v):
+            snd1[zi, t] = coded(v, scale1)
 
         partial_sums(j, store)
         remote(snd1.at[zi], rs1.at[zi], rs1_s.at[zi], rs1_r.at[zi], {"ref": partner}).start()
@@ -259,7 +252,9 @@
     lse_all = jnp.zeros((pos, LANES), f32)
     picked_all = jnp.zeros((pos, LANES), f32)
     for t in range(texts):
-        summed = pltpu.roll(keep[z, t], lax.rem(wl - shift, wl), 1)[:, :piece]
+        both = keep[z, t]
+        summed = jnp.concatenate([both[:pos], both[pos:]], axis=1)
+        summed = pltpu.roll(summed, lax.rem(wl - shift, wl), 1)[:, :piece]
         root = jnp.sqrt(jnp.full((pos, LANES), counts[t].astype(f32), f32))
         factor = (1.0 / (clip_bound * root))[:, :1]
         combined = pub[t].astype(f32) + summed * factor + noise[t].astype(f32)
@@ -339,7 +334,9 @@
     win = max(-(-((j * piece) % LANES + piece) // LANES) for j in range(n))
     while min(j * piece - LANES * min(j * piece // LANES, full + 1 - win) for j in range(n)) < 0:
         win += 1
+    win += win % 2
     wl = win * LANES
+    hl = wl // 2
     bf16, f32, i16 = jnp.bfloat16, jnp.float32, jnp.int16
     smem = pl.BlockSpec(memory_space=pltpu.SMEM)
     vmem = pl.BlockSpec(memory_space=pltpu.VMEM)
@@ -356,18 +353,18 @@
             pltpu.VMEM((rows, pos, width), bf16),
             pltpu.VMEM((rows, pos, n * LANES), bf16),
             pltpu.VMEM((texts, pos, wl), f32),
-            pltpu.VMEM((n, texts, pos, wl), bf16),
-            pltpu.VMEM((texts, pos, wl), f32),
-            pltpu.VMEM((rows + 1, pos, 8 * LANES), f32),
-            pltpu.VMEM((half, texts, pos, wl), f32),
-            pltpu.VMEM((half, texts, pos, wl), i16),
-            pltpu.VMEM((half, texts, pos, wl), i16),
-            pltpu.VMEM((half, texts, pos, wl), i16),
-            pltpu.VMEM((half, texts, pos, wl), i16),
-            pltpu.VMEM((n, 8, LANES), jnp.int32),
+            pltpu.VMEM((n, texts, 2 * pos, hl), bf16),
+            pltpu.VMEM((texts, 2 * pos, hl), f32),
+            pltpu.VMEM((rows + 1, 2 * pos, hl), f32),
+            pltpu.VMEM((half, texts, 2 * pos, hl), f32),
+            pltpu.VMEM((half, texts, 2 * pos, hl), i16),
+            pltpu.VMEM((half, texts, 2 * pos, hl), i16),
+            pltpu.VMEM((half, texts, 2 * pos, hl), i16),
+            pltpu.VMEM((half, texts, 2 * pos, hl), i16),
+            pltpu.VMEM((n, 2 * pos, LANES), jnp.int32),
             pltpu.VMEM((nv, 2 * pos, LANES), f32),
             pltpu.VMEM((n, 2 * pos, LANES), f32),
-            pltpu.VMEM((rows, pos, LANES), f32),
+            pltpu.VMEM((rows, 2 * pos, LANES), f32),
             pltpu.SMEM((rows,), jnp.int32),
             pltpu.SMEM((rows,), jnp.int32),
             pltpu.SMEM((texts + 1,), jnp.int32),

time: 52.1 us -> 52 us (level)
  no operation moved by 1% of the time
where the time goes in v4:
time: 52 us; the launch traced here: 51.8 us
  Pallas kernels  51.2 us (98%)
  between operations  0.64 us (1%)
    pallas_call x1, Pallas kernels, body(): pl.pallas_call(functools.partial(kernel, n, nv, rows, texts, pos, width,...  49.4 us
    pallas_call x1, Pallas kernels, body(): pl.pallas_call(functools.partial(finish, texts, pos), out_shape=(jax.Shap...  1.75 us

profile of v4, /device:TPU:0, one launch (start us, length us, event | category | flops | bytes accessed | tf_op | source)
XLA Modules:
  0.0 51.8 jit_solution(12550552080993200246)
XLA Ops:
  0.6 49.4 %private_scores.1 = (f32[4,4,4008]{2,1,0:T(4,128)}, f32[2,4,128]{2,1,0:T(4,128)}) custom-call(s32[12]{0:T(128)} %owner.1, s32[4]{0:T(128)} %counts.1, s32[4,4]{1,0:T(4,128)} %tokens.1, bf16[12,4,32064]{2,1,0:T(4,128)(2,1)} %priv.1, bf16[4,4,4008]{2,1,0:T(4,128)(2,1)} %pub.1, bf16[4,4,4008]{2,1,0:T(4,128)(2,1)} %noise.1), custom_call_target="tpu_custom_call" | custom-call | flops 9234432 | bytes 3078144 | tf_op jit(solution)/shard_map/private_scores/pallas_call | solution.py:344
  50.1 1.8 %subtract_lse.1 = (f32[4,4,4008]{2,1,0:T(4,128)}, f32[4,4]{1,0:T(4,128)}) custom-call(f32[4,4,4008]{2,1,0:T(4,128)} %get-tuple-element.4.combined, f32[2,4,128]{2,1,0:T(4,128)} %get-tuple-element.5.stats), custom_call_target="tpu_custom_call" | custom-call | tf_op jit(solution)/shard_map/subtract_lse/pallas_call | solution.py:384

commit v5 on v4

--- a/solution.py
+++ b/solution.py
@@ -19,13 +19,18 @@
     return float(scale)
 
 
+def turned(pairs):
+    return (pairs + 3) // 6
+
+
 def kernel(
     n, nv, rows, texts, pos, width, piece, win,
     owner, counts, tokens, priv, pub, noise,
     combined_out, stats_out,
-    pv, xt, pubf, pubs, here, pref, keep, snd1, rs1, snd2, rs2,
+    pv, xt, pubf, pubs, here, pref, keep, snd1, rs1, snd2, rs2, rowb, sndb, rsb, sndf, rsf,
     hist, st1, st2, bnd, order, sown, start,
-    priv_sem, hist_s, hist_r, ag_x, ag_up, ag_dn, ag_r, rs1_s, rs1_r, rs2_s, rs2_r,
+    priv_sem, hist_s, hist_r, ag_x, ag_up, ag_dn, ag_r, agb_up, agb_dn, agb_r,
+    rs1_s, rs1_r, rs2_s, rs2_r, rsb_s, rsb_r, rsf_s, rsf_r,
     st1_s, st1_r, st2_s, st2_r,
 ):
     f32 = jnp.float32
@@ -34,13 +39,15 @@
     wl = win * LANES
     pairs = win // 2
     hl = pairs * LANES
+    hb = turned(pairs) * LANES
     me = lax.axis_index("ref")
     mv = lax.axis_index("voc")
     z = lax.div(me, 2)
     x = lax.rem(me, 2)
     partner = me + 1 - 2 * x
     scale1 = fixed_point(rows)
-    scale2 = fixed_point(2 * rows)
+    scale2 = fixed_point(min(2 * rows, n * rows // texts))
+    scale3 = fixed_point(min(half * rows, n * rows // texts))
 
     def first_tile(j):
         return jnp.minimum(lax.div(j * piece, LANES), full + 1 - win)
@@ -84,24 +91,38 @@
 
     pl.semaphore_wait(barrier, n - 1 + nv - 1)
 
-    def pass_on(zi):
-        j = 2 * zi + x
-        remote(pubs.at[j], pubs.at[j], ag_x.at[zi], ag_r.at[j], {"ref": partner}).start()
-
+    def whole(j):
+        return pubs.at[j]
+
+    def straight(j):
+        return pubs.at[j, :, :, pl.ds(hb, hl - hb)]
+
+    def turning(j):
+        return pubs.at[j, :, :, pl.ds(0, hb)]
+
+    def to_partner(part, j, zi):
+        return remote(part(j), part(j), ag_x.at[zi], ag_r.at[j], {"ref": partner})
+
+    def along(part, j, zi, up, down, recv):
         @pl.when((zi <= z) & (z < half - 1))
         def _():
-            remote(pubs.at[j], pubs.at[j], ag_up.at[zi], ag_r.at[j], {"ref": me + 2}).start()
+            remote(part(j), part(j), up.at[zi], recv, {"ref": me + 2}).start()
 
         @pl.when((zi >= z) & (z > 0))
         def _():
-            remote(pubs.at[j], pubs.at[j], ag_dn.at[zi], ag_r.at[j], {"ref": me - 2}).start()
+            remote(part(j), part(j), down.at[zi], recv, {"ref": me - 2}).start()
+
+    def pass_turned(zi):
+        j = 2 * zi + 1 - x
+        along(turning, j, zi, agb_up, agb_dn, agb_r.at[zi])
 
     def send_hist(k, c):
         remote(hist.at[me], hist.at[me], hist_s, hist_r, {"ref": lax.rem(me + k, n)}).start()
         return c
 
     lax.fori_loop(1, n, send_hist, 0)
-    pass_on(z)
+    to_partner(whole, me, z).start()
+    along(whole, me, z, ag_up, ag_dn, ag_r.at[me])
 
     begin = [jnp.int32(0)]
     for t in range(texts):
@@ -190,52 +211,68 @@
 
         partial_sums(2 * zi + x, store)
 
+    def take_turned(i):
+        zi = column(i)
+        part = turning(2 * zi + 1 - x)
+        remote(part, part, agb_up.at[zi], agb_r.at[zi], {"ref": partner}).wait_recv()
+        pass_turned(zi)
+
     def arrive(i, c):
         zi = column(i)
         j = 2 * zi + x
-        remote(pubs.at[j], pubs.at[j], ag_x.at[zi], ag_r.at[j], {"ref": partner}).wait_recv()
-        pass_on(zi)
+        to_partner(whole, j, zi).wait_recv()
+        to_partner(straight, j, zi).start()
+        along(whole, j, zi, ag_up, ag_dn, ag_r.at[j])
 
         @pl.when(i >= 2)
         def _():
             own_column(i - 1)
+            take_turned(i - 1)
 
         return c
 
     def other_column(i, c):
         zi = column(lax.rem(i, half))
         j = 2 * zi + 1 - x
-        remote(pubs.at[j], pubs.at[j], ag_x.at[zi], ag_r.at[j], {"ref": partner}).wait_recv()
+
+        @pl.when(i < half)
+        def _():
+            to_partner(straight, j, zi).wait_recv()
 
         def store(t, v):
-            snd1[zi, t] = coded(v, scale1)
+            snd1[zi, t] = coded(v[:, hb:], scale1)
+            sndb[zi, t] = coded(v[:, :hb], scale1)
+            rowb[t] = v[:, :hb]
 
         partial_sums(j, store)
         remote(snd1.at[zi], rs1.at[zi], rs1_s.at[zi], rs1_r.at[zi], {"ref": partner}).start()
+
+        @pl.when(i < half)
+        def _():
+            remote(sndb.at[zi], rsb.at[z], rsb_s.at[zi], rsb_r.at[z], {"ref": 2 * zi + x}).start()
+
         return c
 
     def add_partner(i, c):
         zi = column(lax.rem(i, half))
         remote(snd1.at[zi], rs1.at[zi], rs1_s.at[zi], rs1_r.at[zi], {"ref": partner}).wait_recv()
-
-        @pl.when(i == half)
+        for t in range(texts):
+            keep[zi, t, :, hb:] = keep[zi, t, :, hb:] + decoded(rs1[zi, t], scale1)
+
+        @pl.when(i < half)
         def _():
             for t in range(texts):
-                keep[zi, t] = keep[zi, t] + decoded(rs1[zi, t], scale1)
-
-        @pl.when(i < half)
-        def _():
-            for t in range(texts):
-                snd2[zi, t] = coded(keep[zi, t] + decoded(rs1[zi, t], scale1), scale2)
+                snd2[zi, t] = coded(keep[zi, t], scale2)
             remote(snd2.at[zi], rs2.at[z], rs2_s.at[zi], rs2_r.at[z], {"ref": 2 * zi + x}).start()
 
         return c
 
-    own_column(jnp.int32(0))
-    lax.fori_loop(1, half, arrive, 0)
-    lax.fori_loop(1, half + 1, other_column, 0)
-    own_column(jnp.int32(half - 1))
-    lax.fori_loop(1, half + 1, add_partner, 0)
+    def add_turned(k, c):
+        zi = lax.rem(z + k, half)
+        remote(sndb.at[zi], rsb.at[zi], rsb_s.at[zi], rsb_r.at[zi], {"ref": 2 * zi + x}).wait_recv()
+        for t in range(texts):
+            rowb[t] = rowb[t] + decoded(rsb[zi, t], scale1)
+        return c
 
     def gather(k, c):
         zi = lax.rem(z + k, half)
@@ -244,7 +281,23 @@
             keep[z, t] = keep[z, t] + decoded(rs2[zi, t], scale2)
         return c
 
+    own_column(jnp.int32(0))
+    to_partner(whole, 2 * z + 1 - x, z).wait_recv()
+    pass_turned(z)
+    lax.fori_loop(1, half, arrive, 0)
+    take_turned(jnp.int32(half - 1))
+    lax.fori_loop(1, half + 1, other_column, 0)
+    own_column(jnp.int32(half - 1))
+    lax.fori_loop(1, half + 1, add_partner, 0)
+    lax.fori_loop(1, half, add_turned, 0)
+    for t in range(texts):
+        sndf[t] = coded(rowb[t], scale3)
+    last = remote(sndf, rsf, rsf_s, rsf_r, {"ref": partner})
+    last.start()
     lax.fori_loop(1, half, gather, 0)
+    last.wait_recv()
+    for t in range(texts):
+        keep[z, t, :, :hb] = keep[z, t, :, :hb] + decoded(rsf[t], scale3)
 
     first_column = (mv * n + me) * piece
     at_column = lax.broadcasted_iota(jnp.int32, (pos, piece), 1) + first_column
@@ -294,24 +347,32 @@
     stats_out[0] = lse
     stats_out[1] = picked
 
+    def left(src, sem):
+        remote(src, src, sem, ag_r.at[me], {"ref": partner}).wait_send()
+
     def sent(i, c):
-        remote(pubs.at[me], pubs.at[me], ag_x.at[i], ag_r.at[me], {"ref": partner}).wait_send()
-        remote(snd1.at[i], rs1.at[i], rs1_s.at[i], rs1_r.at[i], {"ref": partner}).wait_send()
+        left(snd1.at[i], rs1_s.at[i])
 
         @pl.when((i <= z) & (z < half - 1))
         def _():
-            remote(pubs.at[me], pubs.at[me], ag_up.at[i], ag_r.at[me], {"ref": partner}).wait_send()
+            left(whole(me), ag_up.at[i])
+            left(turning(me), agb_up.at[i])
 
         @pl.when((i >= z) & (z > 0))
         def _():
-            remote(pubs.at[me], pubs.at[me], ag_dn.at[i], ag_r.at[me], {"ref": partner}).wait_send()
+            left(whole(me), ag_dn.at[i])
+            left(turning(me), agb_dn.at[i])
 
         @pl.when(i != z)
         def _():
-            remote(snd2.at[i], rs2.at[i], rs2_s.at[i], rs2_r.at[i], {"ref": partner}).wait_send()
-
-        return c
-
+            left(straight(me), ag_x.at[i])
+            left(snd2.at[i], rs2_s.at[i])
+            left(sndb.at[i], rsb_s.at[i])
+
+        return c
+
+    left(whole(me), ag_x.at[z])
+    left(sndf, rsf_s)
     lax.fori_loop(0, half, sent, 0)
 
 
@@ -337,6 +398,7 @@
     win += win % 2
     wl = win * LANES
     hl = wl // 2
+    hb = turned(win // 2) * LANES
     bf16, f32, i16 = jnp.bfloat16, jnp.float32, jnp.int16
     smem = pl.BlockSpec(memory_space=pltpu.SMEM)
     vmem = pl.BlockSpec(memory_space=pltpu.VMEM)
@@ -357,10 +419,15 @@
             pltpu.VMEM((texts, 2 * pos, hl), f32),
             pltpu.VMEM((rows + 1, 2 * pos, hl), f32),
             pltpu.VMEM((half, texts, 2 * pos, hl), f32),
+            pltpu.VMEM((half, texts, 2 * pos, hl - hb), i16),
+            pltpu.VMEM((half, texts, 2 * pos, hl - hb), i16),
             pltpu.VMEM((half, texts, 2 * pos, hl), i16),
             pltpu.VMEM((half, texts, 2 * pos, hl), i16),
-            pltpu.VMEM((half, texts, 2 * pos, hl), i16),
-            pltpu.VMEM((half, texts, 2 * pos, hl), i16),
+            pltpu.VMEM((texts, 2 * pos, hb), f32),
+            pltpu.VMEM((half, texts, 2 * pos, hb), i16),
+            pltpu.VMEM((half, texts, 2 * pos, hb), i16),
+            pltpu.VMEM((texts, 2 * pos, hb), i16),
+            pltpu.VMEM((texts, 2 * pos, hb), i16),
             pltpu.VMEM((n, 2 * pos, LANES), jnp.int32),
             pltpu.VMEM((nv, 2 * pos, LANES), f32),
             pltpu.VMEM((n, 2 * pos, LANES), f32),
@@ -370,7 +437,9 @@
             pltpu.SMEM((texts + 1,), jnp.int32),
             dma, dma, dma,
             dma((half,)), dma((half,)), dma((half,)), dma((n,)),
+            dma((half,)), dma((half,)), dma((half,)),
             dma((half,)), dma((half,)), dma((half,)), dma((half,)),
+            dma((half,)), dma((half,)), dma, dma,
             dma, dma, dma, dma,
         ],
         compiler_params=pltpu.CompilerParams(

time: 52 us -> 50.4 us (0.969)
  Pallas kernels: 51.2 us -> 49.6 us
    pallas_call x1, Pallas kernels: 49.4 us -> 47.8 us  [body(): pl.pallas_call(functools.partial(kernel, n, nv, rows, texts, pos, width,...]
where the time goes in v5:
time: 50.4 us; the launch traced here: 50.2 us
  Pallas kernels  49.6 us (98%)
  between operations  0.64 us (1%)
    pallas_call x1, Pallas kernels, body(): pl.pallas_call(functools.partial(kernel, n, nv, rows, texts, pos, width,...  47.8 us
    pallas_call x1, Pallas kernels, body(): pl.pallas_call(functools.partial(finish, texts, pos), out_shape=(jax.Shap...  1.75 us

profile of v5, /device:TPU:0, one launch (start us, length us, event | category | flops | bytes accessed | tf_op | source)
XLA Modules:
  0.0 50.2 jit_solution(13335673708467583045)
XLA Ops:
  0.6 47.8 %private_scores.1 = (f32[4,4,4008]{2,1,0:T(4,128)}, f32[2,4,128]{2,1,0:T(4,128)}) custom-call(s32[12]{0:T(128)} %owner.1, s32[4]{0:T(128)} %counts.1, s32[4,4]{1,0:T(4,128)} %tokens.1, bf16[12,4,32064]{2,1,0:T(4,128)(2,1)} %priv.1, bf16[4,4,4008]{2,1,0:T(4,128)(2,1)} %pub.1, bf16[4,4,4008]{2,1,0:T(4,128)(2,1)} %noise.1), custom_call_target="tpu_custom_call" | custom-call | flops 9234432 | bytes 3078144 | tf_op jit(solution)/shard_map/private_scores/pallas_call | solution.py:406
  48.4 1.8 %subtract_lse.1 = (f32[4,4,4008]{2,1,0:T(4,128)}, f32[4,4]{1,0:T(4,128)}) custom-call(f32[4,4,4008]{2,1,0:T(4,128)} %get-tuple-element.4.combined, f32[2,4,128]{2,1,0:T(4,128)} %get-tuple-element.5.stats), custom_call_target="tpu_custom_call" | custom-call | tf_op jit(solution)/shard_map/subtract_lse/pallas_call | solution.py:453

commit v6 on v5

--- a/solution.py
+++ b/solution.py
@@ -26,12 +26,12 @@
 def kernel(
     n, nv, rows, texts, pos, width, piece, win,
     owner, counts, tokens, priv, pub, noise,
-    combined_out, stats_out,
-    pv, xt, pubf, pubs, here, pref, keep, snd1, rs1, snd2, rs2, rowb, sndb, rsb, sndf, rsf,
+    combined_hbm, stats_out,
+    combined_out,    pv, xt, pubf, pubs, here, pref, keep, snd1, rs1, snd2, rs2, rowb, sndb, rsb, sndf, rsf,
     hist, st1, st2, bnd, order, sown, start,
     priv_sem, hist_s, hist_r, ag_x, ag_up, ag_dn, ag_r, agb_up, agb_dn, agb_r,
     rs1_s, rs1_r, rs2_s, rs2_r, rsb_s, rsb_r, rsf_s, rsf_r,
-    st1_s, st1_r, st2_s, st2_r,
+    st1_s, st1_r, st2_s, st2_r, out_sem,
 ):
     f32 = jnp.float32
     half = n // 2
@@ -217,6 +217,28 @@
         remote(part, part, agb_up.at[zi], agb_r.at[zi], {"ref": partner}).wait_recv()
         pass_turned(zi)
 
+    def other_column(i, c):
+        zi = column(lax.rem(i, half))
+        j = 2 * zi + 1 - x
+
+        @pl.when(i < half)
+        def _():
+            to_partner(straight, j, zi).wait_recv()
+
+        def store(t, v):
+            snd1[zi, t] = coded(v[:, hb:], scale1)
+            sndb[zi, t] = coded(v[:, :hb], scale1)
+            rowb[t] = v[:, :hb]
+
+        partial_sums(j, store)
+        remote(snd1.at[zi], rs1.at[zi], rs1_s.at[zi], rs1_r.at[zi], {"ref": partner}).start()
+
+        @pl.when(i < half)
+        def _():
+            remote(sndb.at[zi], rsb.at[z], rsb_s.at[zi], rsb_r.at[z], {"ref": 2 * zi + x}).start()
+
+        return c
+
     def arrive(i, c):
         zi = column(i)
         j = 2 * zi + x
@@ -226,35 +248,18 @@
 
         @pl.when(i >= 2)
         def _():
-            own_column(i - 1)
             take_turned(i - 1)
-
-        return c
-
-    def other_column(i, c):
-        zi = column(lax.rem(i, half))
-        j = 2 * zi + 1 - x
-
-        @pl.when(i < half)
-        def _():
-            to_partner(straight, j, zi).wait_recv()
-
-        def store(t, v):
-            snd1[zi, t] = coded(v[:, hb:], scale1)
-            sndb[zi, t] = coded(v[:, :hb], scale1)
-            rowb[t] = v[:, :hb]
-
-        partial_sums(j, store)
-        remote(snd1.at[zi], rs1.at[zi], rs1_s.at[zi], rs1_r.at[zi], {"ref": partner}).start()
-
-        @pl.when(i < half)
-        def _():
-            remote(sndb.at[zi], rsb.at[z], rsb_s.at[zi], rsb_r.at[z], {"ref": 2 * zi + x}).start()
+            other_column(i - 1, 0)
 
         return c
 
     def add_partner(i, c):
         zi = column(lax.rem(i, half))
+
+        @pl.when(i < half)
+        def _():
+            own_column(i)
+
         remote(snd1.at[zi], rs1.at[zi], rs1_s.at[zi], rs1_r.at[zi], {"ref": partner}).wait_recv()
         for t in range(texts):
             keep[zi, t, :, hb:] = keep[zi, t, :, hb:] + decoded(rs1[zi, t], scale1)
@@ -286,8 +291,7 @@
     pass_turned(z)
     lax.fori_loop(1, half, arrive, 0)
     take_turned(jnp.int32(half - 1))
-    lax.fori_loop(1, half + 1, other_column, 0)
-    own_column(jnp.int32(half - 1))
+    lax.fori_loop(half - 1, half + 1, other_column, 0)
     lax.fori_loop(1, half + 1, add_partner, 0)
     lax.fori_loop(1, half, add_turned, 0)
     for t in range(texts):
@@ -321,6 +325,9 @@
         lse_all = jnp.where(lane4 == t, peak + jnp.log(total), lse_all)
         picked_all = jnp.where(lane4 == t, picked, picked_all)
 
+    out = pltpu.make_async_copy(combined_out, combined_hbm, out_sem)
+    out.start()
+
     def exchange(slots, send, recv, index, count, axis, lse, picked):
         slots[index, :pos] = lse
         slots[index, pos:2 * pos] = picked
@@ -346,6 +353,7 @@
     lse, picked = exchange(st2, st2_s, st2_r, me, n, "ref", lse, picked)
     stats_out[0] = lse
     stats_out[1] = picked
+    out.wait()
 
     def left(src, sem):
         remote(src, src, sem, ag_r.at[me], {"ref": partner}).wait_send()
@@ -410,8 +418,9 @@
             jax.ShapeDtypeStruct((2, pos, LANES), f32),
         ),
         in_specs=[smem, smem, smem, pl.BlockSpec(memory_space=pl.ANY), vmem, vmem],
-        out_specs=(vmem, vmem),
+        out_specs=(pl.BlockSpec(memory_space=pl.ANY), vmem),
         scratch_shapes=[
+            pltpu.VMEM((texts, pos, piece), f32),
             pltpu.VMEM((rows, pos, width), bf16),
             pltpu.VMEM((rows, pos, n * LANES), bf16),
             pltpu.VMEM((texts, pos, wl), f32),
@@ -440,7 +449,7 @@
             dma((half,)), dma((half,)), dma((half,)),
             dma((half,)), dma((half,)), dma((half,)), dma((half,)),
             dma((half,)), dma((half,)), dma, dma,
-            dma, dma, dma, dma,
+            dma, dma, dma, dma, dma,
         ],
         compiler_params=pltpu.CompilerParams(
             collective_id=0, has_side_effects=True, vmem_limit_bytes=56 * 1024 * 1024

time: 50.4 us -> 50.5 us (level)
  no operation moved by 1% of the time
where the time goes in v6:
time: 50.5 us; the launch traced here: 50.4 us
  Pallas kernels  49.7 us (98%)
  between operations  0.64 us (1%)
    pallas_call x1, Pallas kernels, body(): pl.pallas_call(functools.partial(kernel, n, nv, rows, texts, pos, width,...  48 us
    pallas_call x1, Pallas kernels, body(): pl.pallas_call(functools.partial(finish, texts, pos), out_shape=(jax.Shap...  1.75 us

profile of v6, /device:TPU:0, one launch (start us, length us, event | category | flops | bytes accessed | tf_op | source)
XLA Modules:
  0.0 50.4 jit_solution(10140123843552680008)
XLA Ops:
  0.6 48.0 %private_scores.1 = (f32[4,4,4008]{2,1,0:T(4,128)}, f32[2,4,128]{2,1,0:T(4,128)}) custom-call(s32[12]{0:T(128)} %owner.1, s32[4]{0:T(128)} %counts.1, s32[4,4]{1,0:T(4,128)} %tokens.1, bf16[12,4,32064]{2,1,0:T(4,128)(2,1)} %priv.1, bf16[4,4,4008]{2,1,0:T(4,128)(2,1)} %pub.1, bf16[4,4,4008]{2,1,0:T(4,128)(2,1)} %noise.1), custom_call_target="tpu_custom_call" | custom-call | flops 9234432 | bytes 3078144 | tf_op jit(solution)/shard_map/private_scores/pallas_call | solution.py:414
  48.6 1.8 %subtract_lse.1 = (f32[4,4,4008]{2,1,0:T(4,128)}, f32[4,4]{1,0:T(4,128)}) custom-call(f32[4,4,4008]{2,1,0:T(4,128)} %get-tuple-element.4.combined, f32[2,4,128]{2,1,0:T(4,128)} %get-tuple-element.5.stats), custom_call_target="tpu_custom_call" | custom-call | tf_op jit(solution)/shard_map/subtract_lse/pallas_call | solution.py:462

commit v7 on v6

--- a/solution.py
+++ b/solution.py
@@ -172,21 +172,19 @@
         base = first_tile(j) * LANES
         for t in range(texts):
             here[t] = pubs[j, t].astype(f32)
-        acc = [jnp.zeros((2 * pos, LANES), f32)] * pairs
+        base = pl.multiple_of(base, LANES)
+        middle = pl.multiple_of(base + hl, LANES)
+        end = pl.multiple_of(j * LANES, LANES)
+        acc = jnp.zeros((2 * pos, hl), f32)
         for k in range(rows):
             row = order[k]
-            text = sown[k]
-            b = bnd[k]
-            for c in range(pairs):
-                low = pv[row, :, pl.ds(pl.multiple_of(base + c * LANES, LANES), LANES)]
-                if c < pairs - 1:
-                    high = pv[row, :, pl.ds(pl.multiple_of(base + hl + c * LANES, LANES), LANES)]
-                else:
-                    high = xt[row, :, pl.ds(pl.multiple_of(j * LANES, LANES), LANES)]
-                p = jnp.concatenate([low.astype(f32), high.astype(f32)], axis=0)
-                u = here[text, :, c * LANES:(c + 1) * LANES]
-                acc[c] = acc[c] + jnp.minimum(jnp.maximum(p - u, -b), b)
-                pref[k + 1, :, c * LANES:(c + 1) * LANES] = acc[c]
+            b = jnp.concatenate([bnd[k]] * pairs, axis=1)
+            low = pv[row, :, pl.ds(base, hl)].astype(f32)
+            high = pv[row, :, pl.ds(middle, hl - LANES)].astype(f32)
+            high = jnp.concatenate([high, xt[row, :, pl.ds(end, LANES)].astype(f32)], axis=1)
+            p = jnp.concatenate([low, high], axis=0)
+            acc = acc + jnp.minimum(jnp.maximum(p - here[sown[k]], -b), b)
+            pref[k + 1] = acc
         for t in range(texts):
             store(t, pref[start[t + 1]] - pref[start[t]])
 

time: 50.5 us -> 50.1 us (level)
  no operation moved by 1% of the time
where the time goes in v7:
time: 50.1 us; the launch traced here: 50 us
  Pallas kernels  49.3 us (98%)
  between operations  0.64 us (1%)
    pallas_call x1, Pallas kernels, body(): pl.pallas_call(functools.partial(kernel, n, nv, rows, texts, pos, width,...  47.6 us
    pallas_call x1, Pallas kernels, body(): pl.pallas_call(functools.partial(finish, texts, pos), out_shape=(jax.Shap...  1.75 us

profile of v7, /device:TPU:0, one launch (start us, length us, event | category | flops | bytes accessed | tf_op | source)
XLA Modules:
  0.0 50.0 jit_solution(4761978601835282411)
XLA Ops:
  0.6 47.6 %private_scores.1 = (f32[4,4,4008]{2,1,0:T(4,128)}, f32[2,4,128]{2,1,0:T(4,128)}) custom-call(s32[12]{0:T(128)} %owner.1, s32[4]{0:T(128)} %counts.1, s32[4,4]{1,0:T(4,128)} %tokens.1, bf16[12,4,32064]{2,1,0:T(4,128)(2,1)} %priv.1, bf16[4,4,4008]{2,1,0:T(4,128)(2,1)} %pub.1, bf16[4,4,4008]{2,1,0:T(4,128)(2,1)} %noise.1), custom_call_target="tpu_custom_call" | custom-call | flops 9234432 | bytes 3078144 | tf_op jit(solution)/shard_map/private_scores/pallas_call | solution.py:412
  48.2 1.8 %subtract_lse.1 = (f32[4,4,4008]{2,1,0:T(4,128)}, f32[4,4]{1,0:T(4,128)}) custom-call(f32[4,4,4008]{2,1,0:T(4,128)} %get-tuple-element.4.combined, f32[2,4,128]{2,1,0:T(4,128)} %get-tuple-element.5.stats), custom_call_target="tpu_custom_call" | custom-call | tf_op jit(solution)/shard_map/subtract_lse/pallas_call | solution.py:460

commit v8 on v7

--- a/solution.py
+++ b/solution.py
@@ -145,29 +145,6 @@
         order[k] = at
         sown[k] = sum((begin[t] <= k).astype(jnp.int32) for t in range(1, texts))
 
-    load.wait()
-    for j in range(n):
-        s = min(j * piece // LANES, full + 1 - win) + win - 1
-        if s < full:
-            xt[:, :, j * LANES:(j + 1) * LANES] = pv[:, :, s * LANES:(s + 1) * LANES]
-        else:
-            xt[:, :, j * LANES:(j + 1) * LANES] = jnp.zeros((rows, pos, LANES), jnp.bfloat16)
-            if width > full * LANES:
-                xt[:, :, j * LANES:j * LANES + width - full * LANES] = pv[:, :, full * LANES:]
-
-    got = hist.at[pl.ds(0, n - 1)]
-    pltpu.make_async_copy(got, got, hist_r).wait()
-    pltpu.make_async_copy(got, got, hist_s).wait()
-    lower = jnp.zeros((2 * pos, LANES), jnp.int32)
-    lower = lax.fori_loop(0, n, lambda j, a: a + jnp.where(j < me, hist[j], 0), lower)
-    lane4 = lane8[:pos]
-    pref[0] = jnp.zeros_like(pref[0])
-    for k in range(rows):
-        text = sown[k]
-        limit = counts[text] - (k - start[text])
-        ok = jnp.where((lane8 == text) & (lower < limit), clip_bound, 0.0)
-        bnd[k] = jnp.broadcast_to(jnp.max(ok, axis=1, keepdims=True), (2 * pos, LANES))
-
     def partial_sums(j, store):
         base = first_tile(j) * LANES
         for t in range(texts):
@@ -253,11 +230,7 @@
 
     def add_partner(i, c):
         zi = column(lax.rem(i, half))
-
-        @pl.when(i < half)
-        def _():
-            own_column(i)
-
+        own_column(lax.rem(i, half))
         remote(snd1.at[zi], rs1.at[zi], rs1_s.at[zi], rs1_r.at[zi], {"ref": partner}).wait_recv()
         for t in range(texts):
             keep[zi, t, :, hb:] = keep[zi, t, :, hb:] + decoded(rs1[zi, t], scale1)
@@ -284,10 +257,34 @@
             keep[z, t] = keep[z, t] + decoded(rs2[zi, t], scale2)
         return c
 
-    own_column(jnp.int32(0))
     to_partner(whole, 2 * z + 1 - x, z).wait_recv()
     pass_turned(z)
-    lax.fori_loop(1, half, arrive, 0)
+    arrive(jnp.int32(1), 0)
+
+    load.wait()
+    for j in range(n):
+        s = min(j * piece // LANES, full + 1 - win) + win - 1
+        if s < full:
+            xt[:, :, j * LANES:(j + 1) * LANES] = pv[:, :, s * LANES:(s + 1) * LANES]
+        else:
+            xt[:, :, j * LANES:(j + 1) * LANES] = jnp.zeros((rows, pos, LANES), jnp.bfloat16)
+            if width > full * LANES:
+                xt[:, :, j * LANES:j * LANES + width - full * LANES] = pv[:, :, full * LANES:]
+
+    got = hist.at[pl.ds(0, n - 1)]
+    pltpu.make_async_copy(got, got, hist_r).wait()
+    pltpu.make_async_copy(got, got, hist_s).wait()
+    lower = jnp.zeros((2 * pos, LANES), jnp.int32)
+    lower = lax.fori_loop(0, n, lambda j, a: a + jnp.where(j < me, hist[j], 0), lower)
+    lane4 = lane8[:pos]
+    pref[0] = jnp.zeros_like(pref[0])
+    for k in range(rows):
+        text = sown[k]
+        limit = counts[text] - (k - start[text])
+        ok = jnp.where((lane8 == text) & (lower < limit), clip_bound, 0.0)
+        bnd[k] = jnp.broadcast_to(jnp.max(ok, axis=1, keepdims=True), (2 * pos, LANES))
+
+    lax.fori_loop(2, half, arrive, 0)
     take_turned(jnp.int32(half - 1))
     lax.fori_loop(half - 1, half + 1, other_column, 0)
     lax.fori_loop(1, half + 1, add_partner, 0)

time: 50.1 us -> 50.4 us (level)
  no operation moved by 1% of the time
where the time goes in v8:
time: 50.4 us; the launch traced here: 50.2 us
  Pallas kernels  49.6 us (98%)
  between operations  0.64 us (1%)
    pallas_call x1, Pallas kernels, body(): pl.pallas_call(functools.partial(kernel, n, nv, rows, texts, pos, width,...  47.8 us
    pallas_call x1, Pallas kernels, body(): pl.pallas_call(functools.partial(finish, texts, pos), out_shape=(jax.Shap...  1.75 us

profile of v8, /device:TPU:0, one launch (start us, length us, event | category | flops | bytes accessed | tf_op | source)
XLA Modules:
  0.0 50.2 jit_solution(3379951180377466329)
XLA Ops:
  0.6 47.8 %private_scores.1 = (f32[4,4,4008]{2,1,0:T(4,128)}, f32[2,4,128]{2,1,0:T(4,128)}) custom-call(s32[12]{0:T(128)} %owner.1, s32[4]{0:T(128)} %counts.1, s32[4,4]{1,0:T(4,128)} %tokens.1, bf16[12,4,32064]{2,1,0:T(4,128)(2,1)} %priv.1, bf16[4,4,4008]{2,1,0:T(4,128)(2,1)} %pub.1, bf16[4,4,4008]{2,1,0:T(4,128)(2,1)} %noise.1), custom_call_target="tpu_custom_call" | custom-call | flops 9234432 | bytes 3078144 | tf_op jit(solution)/shard_map/private_scores/pallas_call | solution.py:409
  48.4 1.8 %subtract_lse.1 = (f32[4,4,4008]{2,1,0:T(4,128)}, f32[4,4]{1,0:T(4,128)}) custom-call(f32[4,4,4008]{2,1,0:T(4,128)} %get-tuple-element.4.combined, f32[2,4,128]{2,1,0:T(4,128)} %get-tuple-element.5.stats), custom_call_target="tpu_custom_call" | custom-call | tf_op jit(solution)/shard_map/subtract_lse/pallas_call | solution.py:457

commit v9 on v8

--- a/solution.py
+++ b/solution.py
@@ -27,10 +27,10 @@
     n, nv, rows, texts, pos, width, piece, win,
     owner, counts, tokens, priv, pub, noise,
     combined_hbm, stats_out,
-    combined_out,    pv, xt, pubf, pubs, here, pref, keep, snd1, rs1, snd2, rs2, rowb, sndb, rsb, sndf, rsf,
+    combined_out,    pv, xt, pubf, pubs, here, pref, keep, snd1, rs1, snd2, rs2,
     hist, st1, st2, bnd, order, sown, start,
     priv_sem, hist_s, hist_r, ag_x, ag_up, ag_dn, ag_r, agb_up, agb_dn, agb_r,
-    rs1_s, rs1_r, rs2_s, rs2_r, rsb_s, rsb_r, rsf_s, rsf_r,
+    rs1_s, rs1_r, rs2_s, rs2_r,
     st1_s, st1_r, st2_s, st2_r, out_sem,
 ):
     f32 = jnp.float32
@@ -47,7 +47,6 @@
     partner = me + 1 - 2 * x
     scale1 = fixed_point(rows)
     scale2 = fixed_point(min(2 * rows, n * rows // texts))
-    scale3 = fixed_point(min(half * rows, n * rows // texts))
 
     def first_tile(j):
         return jnp.minimum(lax.div(j * piece, LANES), full + 1 - win)
@@ -201,16 +200,10 @@
             to_partner(straight, j, zi).wait_recv()
 
         def store(t, v):
-            snd1[zi, t] = coded(v[:, hb:], scale1)
-            sndb[zi, t] = coded(v[:, :hb], scale1)
-            rowb[t] = v[:, :hb]
+            snd1[zi, t] = coded(v, scale1)
 
         partial_sums(j, store)
         remote(snd1.at[zi], rs1.at[zi], rs1_s.at[zi], rs1_r.at[zi], {"ref": partner}).start()
-
-        @pl.when(i < half)
-        def _():
-            remote(sndb.at[zi], rsb.at[z], rsb_s.at[zi], rsb_r.at[z], {"ref": 2 * zi + x}).start()
 
         return c
 
@@ -230,10 +223,14 @@
 
     def add_partner(i, c):
         zi = column(lax.rem(i, half))
-        own_column(lax.rem(i, half))
+
+        @pl.when(i < half)
+        def _():
+            own_column(i)
+
         remote(snd1.at[zi], rs1.at[zi], rs1_s.at[zi], rs1_r.at[zi], {"ref": partner}).wait_recv()
         for t in range(texts):
-            keep[zi, t, :, hb:] = keep[zi, t, :, hb:] + decoded(rs1[zi, t], scale1)
+            keep[zi, t] = keep[zi, t] + decoded(rs1[zi, t], scale1)
 
         @pl.when(i < half)
         def _():
@@ -241,13 +238,10 @@
                 snd2[zi, t] = coded(keep[zi, t], scale2)
             remote(snd2.at[zi], rs2.at[z], rs2_s.at[zi], rs2_r.at[z], {"ref": 2 * zi + x}).start()
 
-        return c
-
-    def add_turned(k, c):
-        zi = lax.rem(z + k, half)
-        remote(sndb.at[zi], rsb.at[zi], rsb_s.at[zi], rsb_r.at[zi], {"ref": 2 * zi + x}).wait_recv()
-        for t in range(texts):
-            rowb[t] = rowb[t] + decoded(rsb[zi, t], scale1)
+        @pl.when(i == 1)
+        def _():
+            own_column(jnp.int32(0))
+
         return c
 
     def gather(k, c):
@@ -288,15 +282,7 @@
     take_turned(jnp.int32(half - 1))
     lax.fori_loop(half - 1, half + 1, other_column, 0)
     lax.fori_loop(1, half + 1, add_partner, 0)
-    lax.fori_loop(1, half, add_turned, 0)
-    for t in range(texts):
-        sndf[t] = coded(rowb[t], scale3)
-    last = remote(sndf, rsf, rsf_s, rsf_r, {"ref": partner})
-    last.start()
     lax.fori_loop(1, half, gather, 0)
-    last.wait_recv()
-    for t in range(texts):
-        keep[z, t, :, :hb] = keep[z, t, :, :hb] + decoded(rsf[t], scale3)
 
     first_column = (mv * n + me) * piece
     at_column = lax.broadcasted_iota(jnp.int32, (pos, piece), 1) + first_column
@@ -370,12 +356,10 @@
         def _():
             left(straight(me), ag_x.at[i])
             left(snd2.at[i], rs2_s.at[i])
-            left(sndb.at[i], rsb_s.at[i])
 
         return c
 
     left(whole(me), ag_x.at[z])
-    left(sndf, rsf_s)
     lax.fori_loop(0, half, sent, 0)
 
 
@@ -401,7 +385,6 @@
     win += win % 2
     wl = win * LANES
     hl = wl // 2
-    hb = turned(win // 2) * LANES
     bf16, f32, i16 = jnp.bfloat16, jnp.float32, jnp.int16
     smem = pl.BlockSpec(memory_space=pltpu.SMEM)
     vmem = pl.BlockSpec(memory_space=pltpu.VMEM)
@@ -423,15 +406,10 @@
             pltpu.VMEM((texts, 2 * pos, hl), f32),
             pltpu.VMEM((rows + 1, 2 * pos, hl), f32),
             pltpu.VMEM((half, texts, 2 * pos, hl), f32),
-            pltpu.VMEM((half, texts, 2 * pos, hl - hb), i16),
-            pltpu.VMEM((half, texts, 2 * pos, hl - hb), i16),
             pltpu.VMEM((half, texts, 2 * pos, hl), i16),
             pltpu.VMEM((half, texts, 2 * pos, hl), i16),
-            pltpu.VMEM((texts, 2 * pos, hb), f32),
-            pltpu.VMEM((half, texts, 2 * pos, hb), i16),
-            pltpu.VMEM((half, texts, 2 * pos, hb), i16),
-            pltpu.VMEM((texts, 2 * pos, hb), i16),
-            pltpu.VMEM((texts, 2 * pos, hb), i16),
+            pltpu.VMEM((half, texts, 2 * pos, hl), i16),
+            pltpu.VMEM((half, texts, 2 * pos, hl), i16),
             pltpu.VMEM((n, 2 * pos, LANES), jnp.int32),
             pltpu.VMEM((nv, 2 * pos, LANES), f32),
             pltpu.VMEM((n, 2 * pos, LANES), f32),
@@ -443,7 +421,6 @@
             dma((half,)), dma((half,)), dma((half,)), dma((n,)),
             dma((half,)), dma((half,)), dma((half,)),
             dma((half,)), dma((half,)), dma((half,)), dma((half,)),
-            dma((half,)), dma((half,)), dma, dma,
             dma, dma, dma, dma, dma,
         ],
         compiler_params=pltpu.CompilerParams(

time: 50.4 us -> 50.5 us (level)
  no operation moved by 1% of the time
where the time goes in v9:
time: 50.5 us; the launch traced here: 50.4 us
  Pallas kernels  49.7 us (98%)
  between operations  0.64 us (1%)
    pallas_call x1, Pallas kernels, body(): pl.pallas_call(functools.partial(kernel, n, nv, rows, texts, pos, width,...  48 us
    pallas_call x1, Pallas kernels, body(): pl.pallas_call(functools.partial(finish, texts, pos), out_shape=(jax.Shap...  1.75 us

profile of v9, /device:TPU:0, one launch (start us, length us, event | category | flops | bytes accessed | tf_op | source)
XLA Modules:
  0.0 50.4 jit_solution(15750224357374918008)
XLA Ops:
  0.6 48.0 %private_scores.1 = (f32[4,4,4008]{2,1,0:T(4,128)}, f32[2,4,128]{2,1,0:T(4,128)}) custom-call(s32[12]{0:T(128)} %owner.1, s32[4]{0:T(128)} %counts.1, s32[4,4]{1,0:T(4,128)} %tokens.1, bf16[12,4,32064]{2,1,0:T(4,128)(2,1)} %priv.1, bf16[4,4,4008]{2,1,0:T(4,128)(2,1)} %pub.1, bf16[4,4,4008]{2,1,0:T(4,128)(2,1)} %noise.1), custom_call_target="tpu_custom_call" | custom-call | flops 9234432 | bytes 3078144 | tf_op jit(solution)/shard_map/private_scores/pallas_call | solution.py:392
  48.6 1.8 %subtract_lse.1 = (f32[4,4,4008]{2,1,0:T(4,128)}, f32[4,4]{1,0:T(4,128)}) custom-call(f32[4,4,4008]{2,1,0:T(4,128)} %get-tuple-element.4.combined, f32[2,4,128]{2,1,0:T(4,128)} %get-tuple-element.5.stats), custom_call_target="tpu_custom_call" | custom-call | tf_op jit(solution)/shard_map/subtract_lse/pallas_call | solution.py:434

commit v10 on v7

--- a/solution.py
+++ b/solution.py
@@ -337,7 +337,6 @@
         lax.fori_loop(1, count, send_one, 0)
         others = slots.at[pl.ds(0, count - 1)]
         pltpu.make_async_copy(others, others, recv).wait()
-        pltpu.make_async_copy(others, others, send).wait()
         top = lax.fori_loop(1, count, lambda j, a: jnp.maximum(a, slots[j, :pos]), slots[0, :pos])
         zero = jnp.zeros((pos, LANES), f32)
         total, found = lax.fori_loop(
@@ -352,6 +351,10 @@
     stats_out[0] = lse
     stats_out[1] = picked
     out.wait()
+
+    for slots, count, send in ((st1, nv, st1_s), (st2, n, st2_s)):
+        others = slots.at[pl.ds(0, count - 1)]
+        pltpu.make_async_copy(others, others, send).wait()
 
     def left(src, sem):
         remote(src, src, sem, ag_r.at[me], {"ref": partner}).wait_send()

time: 50.1 us -> 50.1 us (level)
  no operation moved by 1% of the time
where the time goes in v10:
time: 50.1 us; the launch traced here: 50 us
  Pallas kernels  49.4 us (99%)
  between operations  0.64 us (1%)
    pallas_call x1, Pallas kernels, body(): pl.pallas_call(functools.partial(kernel, n, nv, rows, texts, pos, width,...  47.6 us
    pallas_call x1, Pallas kernels, body(): pl.pallas_call(functools.partial(finish, texts, pos), out_shape=(jax.Shap...  1.75 us

profile of v10, /device:TPU:0, one launch (start us, length us, event | category | flops | bytes accessed | tf_op | source)
XLA Modules:
  0.0 50.0 jit_solution(8795193464549080814)
XLA Ops:
  0.6 47.6 %private_scores.1 = (f32[4,4,4008]{2,1,0:T(4,128)}, f32[2,4,128]{2,1,0:T(4,128)}) custom-call(s32[12]{0:T(128)} %owner.1, s32[4]{0:T(128)} %counts.1, s32[4,4]{1,0:T(4,128)} %tokens.1, bf16[12,4,32064]{2,1,0:T(4,128)(2,1)} %priv.1, bf16[4,4,4008]{2,1,0:T(4,128)(2,1)} %pub.1, bf16[4,4,4008]{2,1,0:T(4,128)(2,1)} %noise.1), custom_call_target="tpu_custom_call" | custom-call | flops 9234432 | bytes 3078144 | tf_op jit(solution)/shard_map/private_scores/pallas_call | solution.py:415
  48.2 1.8 %subtract_lse.1 = (f32[4,4,4008]{2,1,0:T(4,128)}, f32[4,4]{1,0:T(4,128)}) custom-call(f32[4,4,4008]{2,1,0:T(4,128)} %get-tuple-element.4.combined, f32[2,4,128]{2,1,0:T(4,128)} %get-tuple-element.5.stats), custom_call_target="tpu_custom_call" | custom-call | tf_op jit(solution)/shard_map/subtract_lse/pallas_call | solution.py:463
